TPU v7x, 256 devices: a whole 4x4x8 slice. The times are simulated.
256 devices in a mesh: tower: 8 (over y, x_hi), seq: 16 (over x_lo, z), dp: 2 (over core).
Axes of the slice: x: 4 (x_hi: 2, x_lo: 2; x = x_hi * 2 + x_lo), y: 4, z: 8, core: 2. Of those that a mesh axis runs over, the one named last changes fastest.
Arguments:
- video_query: bfloat16 [2, 8192, 3072], P('dp', 'seq', 'tower'), may hold values from -8 to 8
- audio_key: bfloat16 [2, 1024, 3072], P('dp', 'seq', 'tower'), may hold values from -8 to 8
- audio_value: bfloat16 [2, 1024, 3072], P('dp', 'seq', 'tower'), may hold values from -6 to 6
- audio_query: bfloat16 [2, 1024, 3072], P('dp', 'seq', 'tower'), may hold values from -8 to 8
- video_key: bfloat16 [2, 8192, 3072], P('dp', 'seq', 'tower'), may hold values from -8 to 8
- video_value_rows: bfloat16 [2, 8192, 3072], P('dp', 'seq', 'tower'), may hold values from -6 to 6
- video_upstream: bfloat16 [2, 8192, 3072], P('dp', 'seq', 'tower'), may hold values from -6 to 6
- audio_output_gradient: bfloat16 [2, 1024, 3072], P('dp', 'seq', 'tower'), may hold values from -6 to 6
- gains: float32 [4, 3072], P(None, 'tower'), may hold values from 0.1 to 1.9
- video_lengths: int32 [2], P('dp'), may hold values from 2048 to 8192, as said below
- audio_lengths: int32 [2], P('dp'), may hold values from 256 to 1024, as said below
Outputs:
- video_output: bfloat16 [2, 8192, 3072], P('dp', 'seq', 'tower')
- audio_cross_output: bfloat16 [2, 1024, 3072], P('dp', 'seq', 'tower')
- video_query_grad: bfloat16 [2, 8192, 3072], P('dp', 'seq', 'tower')
- audio_key_grad: bfloat16 [2, 1024, 3072], P('dp', 'seq', 'tower')
- audio_value_grad: bfloat16 [2, 1024, 3072], P('dp', 'seq', 'tower')
- audio_query_grad: bfloat16 [2, 1024, 3072], P('dp', 'seq', 'tower')
- video_key_grad: bfloat16 [2, 8192, 3072], P('dp', 'seq', 'tower')
- video_value_grad: bfloat16 [2, 8192, 3072], P('dp', 'seq', 'tower')
- gain_grads: float32 [4, 3072], P(None, 'tower')
Inputs may be any that keep to these rules, and one draw needn't show every extreme that they name: `video_lengths`: some clip has all 8192 video tokens live. `audio_lengths`: some clip has all 1024 audio tokens live.
All inputs are finite; a program needn't handle non-finite values.
Results may differ from a plain program's by a relative error of at most 0.04.
Values may be sent and summed in bfloat16 or wider, within the bound.
A program may use at most 128 MiB of HBM per device.

v0:
```python
import math

import jax
import jax.numpy as jnp
from jax import lax
from jax.sharding import PartitionSpec as P

HD = 128
D = 3072


epsilon = 1e-06
masked_score = -1e30


def combined_all(value, axis, combine):
    everything = jax.tree.map(lambda part: lax.all_gather(part, axis), value)
    first = jax.tree.map(lambda part: part[0], everything)

    def hop(k, so_far):
        return combine(so_far, jax.tree.map(lambda part: part[k], everything))

    return lax.fori_loop(1, lax.axis_size(axis), hop, first)


def row_power(tensor):
    widened = tensor.astype(jnp.float32)
    return jnp.sum(widened * widened, axis=-1)


def normalize(tensor, factors, gain):
    return (tensor.astype(jnp.float32) * factors[..., None] * gain).astype(jnp.bfloat16)


def divide_heads(tensor):
    return tensor.reshape(tensor.shape[0], tensor.shape[1], tensor.shape[2] // HD, HD)


def merge_heads(tensor):
    return tensor.reshape(tensor.shape[0], tensor.shape[1], tensor.shape[2] * tensor.shape[3])


def combine_partial(former, latter):
    largest = jnp.maximum(former[0], latter[0])
    return (
        largest,
        former[1] * jnp.exp(former[0] - largest) + latter[1] * jnp.exp(latter[0] - largest),
    )


def head_delta(upstream, output):
    products = divide_heads(upstream).astype(jnp.float32) * divide_heads(output).astype(jnp.float32)
    return jnp.transpose(jnp.sum(products, axis=-1), (0, 2, 1))


def norm_back(tensor, factors, gain, upstream, inner_sum):
    widened = tensor.astype(jnp.float32)
    column = factors[..., None]
    gradient = (
        column * gain * upstream - widened * (column * column * column) * inner_sum[..., None] / D
    )
    return gradient.astype(jnp.bfloat16)


def body(
    video_query,
    audio_key,
    audio_value,
    audio_query,
    video_key,
    video_value_rows,
    video_upstream,
    audio_output_gradient,
    gains,
    video_lengths,
    audio_lengths,
):
    score_scale = 1.0 / math.sqrt(HD)
    raw_inputs = (video_query, audio_key, audio_query, video_key)
    powers = lax.psum(
        (
            row_power(video_query),
            row_power(audio_key),
            row_power(audio_query),
            row_power(video_key),
        ),
        "tower",
    )
    factors = [lax.rsqrt(powers[number] / D + epsilon) for number in range(4)]
    video_qnorm = normalize(video_query, factors[0], gains[0])
    audio_knorm = normalize(audio_key, factors[1], gains[1])
    audio_qnorm = normalize(audio_query, factors[2], gains[2])
    video_key_norm = normalize(video_key, factors[3], gains[3])
    audio_keys, audio_values, audio_queries, audio_incoming = (
        lax.all_gather(audio_knorm, "seq", axis=1, tiled=True),
        lax.all_gather(audio_value, "seq", axis=1, tiled=True),
        lax.all_gather(audio_qnorm, "seq", axis=1, tiled=True),
        lax.all_gather(audio_output_gradient, "seq", axis=1, tiled=True),
    )
    audio_count = audio_keys.shape[1]
    audio_alive = lax.broadcasted_iota(jnp.int32, (1, audio_count), 1) < audio_lengths[:, None]
    video_rows = video_key.shape[1]
    video_positions = lax.axis_index("seq") * video_rows + lax.broadcasted_iota(
        jnp.int32, (1, video_rows), 1
    )
    video_valid_mask = video_positions < video_lengths[:, None]
    query_heads = divide_heads(video_qnorm)
    key_heads = divide_heads(audio_keys)
    value_heads = divide_heads(audio_values)
    grad_heads = divide_heads(video_upstream)
    alive_audio = audio_alive[:, None, None, :]
    scores = (
        jnp.einsum("opfb,otfb->ofpt", query_heads, key_heads, preferred_element_type=jnp.float32)
        * score_scale
    )
    scores = jnp.where(alive_audio, scores, masked_score)
    largest = jnp.max(scores, axis=-1, keepdims=True)
    summed = jnp.sum(jnp.where(alive_audio, jnp.exp(scores - largest), 0.0), axis=-1, keepdims=True)
    weights = jnp.where(alive_audio, jnp.exp(scores - (largest + jnp.log(summed))), 0.0)
    weights_low = weights.astype(jnp.bfloat16)
    video_output = merge_heads(
        jnp.einsum("yrgm,ymrx->ygrx", weights_low, value_heads, preferred_element_type=jnp.float32)
    ).astype(jnp.bfloat16)
    video_delta = head_delta(video_upstream, video_output)
    dweights = jnp.einsum(
        "opfb,otfb->ofpt", grad_heads, value_heads, preferred_element_type=jnp.float32
    )
    dscores = (weights * (dweights - video_delta[..., None]) * score_scale).astype(jnp.bfloat16)
    video_query_gradient = merge_heads(
        jnp.einsum("yrgm,ymrx->ygrx", dscores, key_heads, preferred_element_type=jnp.float32)
    )
    part_akey = merge_heads(
        jnp.einsum("chqk,cqhd->ckhd", dscores, query_heads, preferred_element_type=jnp.float32)
    )
    part_avalue = merge_heads(
        jnp.einsum("chqk,cqhd->ckhd", weights_low, grad_heads, preferred_element_type=jnp.float32)
    )
    audio_query_split = divide_heads(audio_queries)
    agrad_heads = divide_heads(audio_incoming)
    video_key_split = divide_heads(video_key_norm)
    vvalue_heads = divide_heads(video_value_rows)
    alive_video = video_valid_mask[:, None, None, :]
    ascores = (
        jnp.einsum(
            "opfb,otfb->ofpt",
            audio_query_split,
            video_key_split,
            preferred_element_type=jnp.float32,
        )
        * score_scale
    )
    ascores = jnp.where(alive_video, ascores, masked_score)
    local_largest = jnp.max(ascores, axis=-1)
    local_summed = jnp.sum(
        jnp.where(alive_video, jnp.exp(ascores - local_largest[..., None]), 0.0), axis=-1
    )
    all_largest, all_summed = combined_all((local_largest, local_summed), "seq", combine_partial)
    log_summed = all_largest + jnp.log(all_summed)
    aweights = jnp.where(alive_video, jnp.exp(ascores - log_summed[..., None]), 0.0)
    aweights_low = aweights.astype(jnp.bfloat16)
    part_output = merge_heads(
        jnp.einsum(
            "yrgm,ymrx->ygrx", aweights_low, vvalue_heads, preferred_element_type=jnp.float32
        )
    )
    audio_rows = audio_query.shape[1]
    first_row = lax.axis_index("seq") * audio_rows
    whole_output = lax.psum(part_output, "seq").astype(jnp.bfloat16)
    audio_cross_output = lax.dynamic_slice_in_dim(whole_output, first_row, audio_rows, 1)
    audio_delta = head_delta(audio_incoming, whole_output)
    adweights = jnp.einsum(
        "opfb,otfb->ofpt", agrad_heads, vvalue_heads, preferred_element_type=jnp.float32
    )
    audio_score_gradient = (aweights * (adweights - audio_delta[..., None]) * score_scale).astype(
        jnp.bfloat16
    )
    part_aquery = merge_heads(
        jnp.einsum(
            "yrgm,ymrx->ygrx",
            audio_score_gradient,
            video_key_split,
            preferred_element_type=jnp.float32,
        )
    )
    video_key_gradient = merge_heads(
        jnp.einsum(
            "chqk,cqhd->ckhd",
            audio_score_gradient,
            audio_query_split,
            preferred_element_type=jnp.float32,
        )
    )
    video_value_grad = merge_heads(
        jnp.einsum("chqk,cqhd->ckhd", aweights_low, agrad_heads, preferred_element_type=jnp.float32)
    ).astype(jnp.bfloat16)
    local_audio_query, local_audio_key, own_avalue = (
        lax.psum_scatter(
            part_aquery.astype(jnp.bfloat16), "seq", scatter_dimension=1, tiled=True
        ).astype(jnp.float32),
        lax.psum_scatter(
            part_akey.astype(jnp.bfloat16), "seq", scatter_dimension=1, tiled=True
        ).astype(jnp.float32),
        lax.psum_scatter(
            part_avalue.astype(jnp.bfloat16), "seq", scatter_dimension=1, tiled=True
        ).astype(jnp.float32),
    )
    audio_value_grad = own_avalue.astype(jnp.bfloat16)
    incoming_gradients = (
        video_query_gradient,
        local_audio_key,
        local_audio_query,
        video_key_gradient,
    )
    inner_local = tuple(
        (
            jnp.sum(
                raw_inputs[number].astype(jnp.float32) * gains[number] * incoming_gradients[number],
                axis=-1,
            )
            for number in range(4)
        )
    )
    gain_local = jnp.stack(
        [
            jnp.sum(
                incoming_gradients[number]
                * raw_inputs[number].astype(jnp.float32)
                * factors[number][..., None],
                axis=(0, 1),
            )
            for number in range(4)
        ]
    )
    inner_sums = lax.psum(inner_local, "tower")
    gain_grads = lax.psum(gain_local, ("seq", "dp"))
    input_grads = [
        norm_back(
            raw_inputs[number],
            factors[number],
            gains[number],
            incoming_gradients[number],
            inner_sums[number],
        )
        for number in range(4)
    ]
    return (
        video_output,
        audio_cross_output,
        input_grads[0],
        input_grads[1],
        audio_value_grad,
        input_grads[2],
        input_grads[3],
        video_value_grad,
        gain_grads,
    )


def solution(mesh):
    return jax.shard_map(
        body,
        mesh=mesh,
        in_specs=(
            P("dp", "seq", "tower"),
            P("dp", "seq", "tower"),
            P("dp", "seq", "tower"),
            P("dp", "seq", "tower"),
            P("dp", "seq", "tower"),
            P("dp", "seq", "tower"),
            P("dp", "seq", "tower"),
            P("dp", "seq", "tower"),
            P(None, "tower"),
            P("dp"),
            P("dp"),
        ),
        out_specs=(
            P("dp", "seq", "tower"),
            P("dp", "seq", "tower"),
            P("dp", "seq", "tower"),
            P("dp", "seq", "tower"),
            P("dp", "seq", "tower"),
            P("dp", "seq", "tower"),
            P("dp", "seq", "tower"),
            P("dp", "seq", "tower"),
            P(None, "tower"),
        ),
        check_vma=False,
    )
```

profile of v0, /device:TPU:8, one launch (start us, length us, event | category | flops | bytes accessed | tf_op | source)
XLA Modules:
  0.0 576.1 jit_solution(11348573041644954611)
XLA Ops:
  16.4 23.1 %all-reduce.1 = (f32[1,512]{1,0:T(1,128)S(1)}, f32[1,64]{1,0:T(1,128)S(1)}, f32[1,64]{1,0:T(1,128)}, f32[1,512]{1,0:T(1,128)}) all-reduce(f32[1,512]{1,0:T(1,128)S(1)} %bitcast.198, f32[1,64]{1,0:T(1,128)S(1)} %bitcast.200, f32[1,64]{1,0:T(1,128)S(1)} %bitcast.201, ...), channel_id=1, replica_groups=mesh['tower'=8,'seq'=16,'dp'=2] {'tower'}, use_global_device_ids=true, to_apply=%region_1.0 | all-reduce | flops 1152 | bytes 9216 | tf_op jit(solution)/shard_map/psum | solution.py:80
  40.9 40.0 %all_gather.24 = bf16[1,1024,384]{2,1,0:T(8,128)(2,1)S(1)} all-gather(bf16[1,64,384]{2,1,0:T(8,128)(2,1)S(1)} %fusion.36), channel_id=1, replica_groups=mesh['tower'=8,'seq'=16,'dp'=2] {'seq'}, dimensions={1}, use_global_device_ids=true | all-gather | bytes 835584 | tf_op jit(solution)/shard_map/all_gather | solution.py:95
  81.2 34.6 %all_gather.25 = bf16[1,1024,384]{2,1,0:T(8,128)(2,1)S(1)} all-gather(bf16[1,64,384]{2,1,0:T(8,128)(2,1)S(1)} %copy-done.26), channel_id=1, replica_groups=mesh['tower'=8,'seq'=16,'dp'=2] {'seq'}, dimensions={1}, use_global_device_ids=true | all-gather | bytes 835584 | tf_op jit(solution)/shard_map/all_gather | solution.py:96
  120.2 2.6 multiply_reduce_fusion
  122.9 2.7 multiply_convert_fusion.1
  127.1 4.8 copy.127
  138.7 38.9 %all_gather.26 = bf16[1,1024,384]{2,1,0:T(8,128)(2,1)} all-gather(bf16[1,64,384]{2,1,0:T(8,128)(2,1)S(1)} %fusion.43), channel_id=1, replica_groups=mesh['tower'=8,'seq'=16,'dp'=2] {'seq'}, dimensions={1}, use_global_device_ids=true | all-gather | bytes 835584 | tf_op jit(solution)/shard_map/all_gather | solution.py:97
  184.2 2.6 copy-done
  188.6 31.5 %all-gather.3 = f32[16,3,1024]{2,1,0:T(4,128)S(1)} all-gather(f32[1,3,1024]{2,1,0:T(4,128)S(1)} %bitcast.188), channel_id=3, replica_groups=mesh['tower'=8,'seq'=16,'dp'=2] {'seq'}, dimensions={0}, use_global_device_ids=true | all-gather | bytes 208896 | tf_op jit(solution)/shard_map/all_gather | solution.py:17
  220.2 32.6 %all-gather.2 = f32[16,3,1024]{2,1,0:T(4,128)S(1)} all-gather(f32[1,3,1024]{2,1,0:T(4,128)S(1)} %bitcast.187), channel_id=2, replica_groups=mesh['tower'=8,'seq'=16,'dp'=2] {'seq'}, dimensions={0}, use_global_device_ids=true | all-gather | bytes 208896 | tf_op jit(solution)/shard_map/all_gather | solution.py:17
  253.5 20.5 %while.17 = (s32[]{:T(128)}, f32[1,3,1024]{2,1,0:T(4,128)}, f32[1,3,1024]{2,1,0:T(4,128)S(1)}, f32[16,1,3,1024]{3,2,1,0:T(4,128)}, f32[16,1,3,1024]{3,2,1,0:T(4,128)}, /*index=5*/s32[]{:T(128)}, s32[]{:T(128)}, s32[]{:T(128)}) while((s32[]{:T(128)}, f32[1,3,1024]{2,1,0:T(4,128)}, f32[1,3,1024]{2,1,0:T(4,128)S(1)}, ...), condition=%wide.region_13.14_spmd, body=%wide.region_12.13_spmd.sunk | while | flops 18437 | bytes 73851 | solution.py:23
  274.8 4.5 fusion.3
  282.7 75.4 %all-reduce.3 = bf16[1,1024,384]{1,2,0:T(8,128)(2,1)} all-reduce(f32[1,1024,384]{1,2,0:T(8,128)} %bitcast.157), channel_id=1, replica_groups=mesh['tower'=8,'seq'=16,'dp'=2] {'seq'}, use_global_device_ids=true, to_apply=%region_14.15 | all-reduce | flops 393216 | bytes 2359296 | tf_op jit(solution)/shard_map/psum | solution.py:168
  358.1 37.7 %all_gather.31 = bf16[1,1024,384]{2,1,0:T(8,128)(2,1)} all-gather(bf16[1,64,384]{2,1,0:T(8,128)(2,1)} %param.20), channel_id=1, replica_groups=mesh['tower'=8,'seq'=16,'dp'=2] {'seq'}, dimensions={1}, use_global_device_ids=true | all-gather | bytes 835584 | tf_op jit(solution)/shard_map/all_gather | solution.py:98
  398.1 2.8 convert_multiply_fusion
  403.0 5.7 multiply_convert_fusion
  411.9 4.8 copy.129
  416.7 2.4 copy.143
  419.5 5.4 convolution_convert_fusion
  429.1 3.2 fusion.50
  432.4 3.4 convolution_convert_fusion.3
  442.9 43.1 %reduce-scatter.12.cloned.1.call-done = bf16[64,384]{1,0:T(8,128)(2,1)} async-done(((bf16[1024,384]{1,0:T(8,128)(2,1)}), bf16[64,384]{1,0:T(8,128)(2,1)}) %reduce-scatter.12.cloned.1.call-update) | async-done | bytes 49168
  487.7 21.8 %all-reduce = (f32[512]{0:T(512)S(1)}, f32[64]{0:T(128)S(1)}, f32[64]{0:T(128)S(1)}, f32[512]{0:T(512)S(1)}) all-reduce(f32[512]{0:T(512)S(1)} %get-tuple-element.177, f32[64]{0:T(128)S(1)} %get-tuple-element.181, f32[64]{0:T(128)S(1)} %get-tuple-element.183, ...), channel_id=1, replica_groups=mesh['tower'=8,'seq'=16,'dp'=2] {'tower'}, use_global_device_ids=true, to_apply=%region_17.18 | all-reduce | flops 1152 | bytes 9216 | tf_op jit(solution)/shard_map/psum | solution.py:234
  512.4 55.7 %psum.79 = f32[4,384]{1,0:T(4,128)} all-reduce(f32[4,384]{1,0:T(4,128)S(1)} %pad_maximum_fusion), channel_id=1, replica_groups=mesh['tower'=8,'seq'=16,'dp'=2] {'seq','dp'}, use_global_device_ids=true, to_apply=%region_32.33 | all-reduce | flops 1536 | bytes 12288 | tf_op jit(solution)/shard_map/psum | solution.py:235
  (176 shorter events, 80.9 us)
Async XLA Ops:
  7.2 74.0 %copy-start.26 = (bf16[1,64,384]{2,1,0:T(8,128)(2,1)S(1)}, bf16[1,64,384]{2,1,0:T(8,128)(2,1)}, u32[]{:S(2)}) copy-start(bf16[1,64,384]{2,1,0:T(8,128)(2,1)} %param.15) | copy-start | bytes 147460
  7.2 434.6 %reduce-scatter.10.cloned.1.call-start = ((), (), s32[]{:S(2)}) async-start(), calls=%async_computation.4 | async-start | bytes 835584
  11.0 111.9 %copy-start.41 = (pred[1024]{0:T(1024)(128)(4,1)}, pred[1024]{0:T(1024)(128)(4,1)S(1)}, u32[]{:S(2)}) copy-start(pred[1024]{0:T(1024)(128)(4,1)S(1)} %iota_compare_fusion) | copy-start | bytes 3076
  13.7 104.6 %copy-start.29 = (f32[384]{0:T(512)}, f32[384]{0:T(512)S(1)}, u32[]{:S(2)}) copy-start(f32[384]{0:T(512)S(1)} %get-tuple-element.186) | copy-start | bytes 4612
  13.7 104.6 %copy-start.31 = (f32[384]{0:T(512)}, f32[384]{0:T(512)S(1)}, u32[]{:S(2)}) copy-start(f32[384]{0:T(512)S(1)} %get-tuple-element.185) | copy-start | bytes 4612
  13.8 124.0 %copy-start.33 = (f32[384]{0:T(512)}, f32[384]{0:T(512)S(1)}, u32[]{:S(2)}) copy-start(f32[384]{0:T(512)S(1)} %get-tuple-element.187) | copy-start | bytes 4612
  13.8 166.1 %copy-start.27 = (f32[384]{0:T(512)}, f32[384]{0:T(512)S(1)}, u32[]{:S(2)}) copy-start(f32[384]{0:T(512)S(1)} %get-tuple-element.184) | copy-start | bytes 4612
  16.2 102.1 %copy-start.5 = (bf16[1,512,384]{1,2,0:T(8,128)(2,1)}, bf16[1,512,384]{1,2,0:T(8,128)(2,1)S(1)}, u32[]{:S(2)}) copy-start(bf16[1,512,384]{1,2,0:T(8,128)(2,1)S(1)} %copy.87) | copy-start | bytes 1179652
  39.5 78.8 %copy-start.22 = (f32[1,512]{1,0:T(1,128)}, f32[1,512]{1,0:T(1,128)S(1)}, u32[]{:S(2)}) copy-start(f32[1,512]{1,0:T(1,128)S(1)} %add_rsqrt_fusion.1) | copy-start | bytes 6148
  40.0 78.4 %copy-start.37 = (f32[64]{0:T(128)}, f32[64]{0:T(128)S(1)}, u32[]{:S(2)}) copy-start(f32[64]{0:T(128)S(1)} %rsqrt_bitcast_fusion.1) | copy-start | bytes 772
  81.1 39.0 %copy-start.7 = (bf16[1,1024,384]{1,2,0:T(8,128)(2,1)}, bf16[1,1024,384]{1,2,0:T(8,128)(2,1)S(1)}, u32[]{:S(2)}) copy-start(bf16[1,1024,384]{1,2,0:T(8,128)(2,1)S(1)} %copy.82) | copy-start | bytes 2359300
  125.6 9.5 %copy-start.43 = (f32[1,64]{1,0:T(1,128)S(1)}, f32[1,64]{1,0:T(1,128)}, u32[]{:S(2)}) copy-start(f32[1,64]{1,0:T(1,128)} %get-tuple-element.204) | copy-start | bytes 772
  134.4 351.5 %reduce-scatter.12.cloned.1.call-start = ((), (), s32[]{:S(2)}) async-start(), calls=%async_computation.5 | async-start | bytes 835584
  135.2 53.5 %copy-start.39 = (f32[64]{0:T(128)}, f32[64]{0:T(128)S(1)}, u32[]{:S(2)}) copy-start(f32[64]{0:T(128)S(1)} %rsqrt_bitcast_fusion) | copy-start | bytes 772
  135.9 52.8 %copy-start.24 = (f32[1,512]{1,0:T(1,128)}, f32[1,512]{1,0:T(1,128)S(1)}, u32[]{:S(2)}) copy-start(f32[1,512]{1,0:T(1,128)S(1)} %add_rsqrt_fusion) | copy-start | bytes 6148
  220.2 33.3 %copy-start.16 = (f32[16,3,1024]{2,1,0:T(4,128)}, f32[16,3,1024]{2,1,0:T(4,128)S(1)}, u32[]{:S(2)}) copy-start(f32[16,3,1024]{2,1,0:T(4,128)S(1)} %all-gather.3) | copy-start | bytes 589828
  282.7 120.3 %copy-start.21 = (f32[3,1024]{1,0:T(4,128)S(1)}, f32[3,1024]{1,0:T(4,128)}, u32[]{:S(2)}) copy-start(f32[3,1024]{1,0:T(4,128)} %copy-done.20) | copy-start | bytes 36868
  419.2 150.4 %reduce-scatter.8.cloned.1.call-start = ((), (), s32[]{:S(2)}) async-start(), calls=%async_computation.3 | async-start | bytes 835584 | tf_op jit(solution)/shard_map/reduce_scatter | solution.py:203
  432.4 9.4 %copy-start.44 = (f32[1,64]{1,0:T(1,128)S(1)}, f32[1,64]{1,0:T(1,128)}, u32[]{:S(2)}) copy-start(f32[1,64]{1,0:T(1,128)} %get-tuple-element.204) | copy-start | bytes 772
  432.4 10.3 %copy-start.14 = (bf16[1,64,384]{2,1,0:T(8,128)(2,1)S(1)}, bf16[1,64,384]{2,1,0:T(8,128)(2,1)}, u32[]{:S(2)}) copy-start(bf16[1,64,384]{2,1,0:T(8,128)(2,1)} %param.14) | copy-start | bytes 147460
  432.4 10.3 %copy-start.32 = (f32[384]{0:T(512)S(1)}, f32[384]{0:T(512)}, u32[]{:S(2)}) copy-start(f32[384]{0:T(512)} %copy-done.31) | copy-start | bytes 4612
  432.4 10.3 %copy-start.38 = (f32[64]{0:T(128)S(1)}, f32[64]{0:T(128)}, u32[]{:S(2)}) copy-start(f32[64]{0:T(128)} %copy-done.37) | copy-start | bytes 772
  432.4 54.4 %copy-start.15 = (bf16[1,64,384]{2,1,0:T(8,128)(2,1)S(1)}, bf16[1,64,384]{2,1,0:T(8,128)(2,1)}, u32[]{:S(2)}) copy-start(bf16[1,64,384]{2,1,0:T(8,128)(2,1)} %param.16) | copy-start | bytes 147460
  441.5 70.9 %copy-start.36 = (f32[1,384]{1,0:T(1,128)S(1)}, f32[1,384]{1,0:T(1,128)}, u32[]{:S(2)}) copy-start(f32[1,384]{1,0:T(1,128)} %stack.15) | copy-start | bytes 4612
  (25 other events, 143.1 us)
Sparse Core Ops, SparseCore 0:
  134.5 66.2 reduce-scatter.9
  419.3 66.5 reduce-scatter.11
  489.0 66.8 reduce-scatter.7
where the time goes:
time: 582 us; the launch traced here: 576 us
  blocking collectives  391 us (67%)
  local copies, waits for them, and re-layouts  46.9 us (8%)
  other arithmetic  46 us (8%)
  waiting for transfers between devices  43.1 us (7%)
  matrix products  32.6 us (6%)
  between operations  15.7 us (3%)
    psum x1, blocking collectives, body(): whole_output = lax.psum(part_output, 'seq').astype(jnp.bfloat16)  75.4 us
    all_gather x2, blocking collectives, combined_all(): everything = jax.tree.map(lambda part: lax.all_gather(part, axis), value)  64.1 us
    psum x1, blocking collectives, body(): gain_grads = lax.psum(gain_local, ('seq', 'dp'))  55.7 us
    unnamed x5, waiting for transfers between devices  43.1 us
    all_gather x1, blocking collectives, body(): lax.all_gather(audio_knorm, 'seq', axis=1, tiled=True)  40 us
    all_gather x1, blocking collectives, body(): lax.all_gather(audio_qnorm, 'seq', axis=1, tiled=True)  38.9 us
    all_gather x1, blocking collectives, body(): lax.all_gather(audio_output_gradient, 'seq', axis=1, tiled=True)  37.7 us
    all_gather x1, blocking collectives, body(): lax.all_gather(audio_value, 'seq', axis=1, tiled=True)  34.6 us
  transfers between devices with their start and end apart: 3, of which 1 were waited for; matrix products, arithmetic and copies ran while one was open for 16% of the time, Pallas kernels for 0%

commit v1 on v0

v1 whole, which is shorter than its diff:
```python
import functools
import math

import jax
import jax.numpy as jnp
from jax import lax
from jax.experimental import pallas as pl
from jax.experimental.pallas import tpu as pltpu
from jax.sharding import PartitionSpec as P

HD = 128
EPS = 1e-06
MASKED = -1e30
FLOOR = -1e29
F32 = jnp.float32
BF16 = jnp.bfloat16

NT = (((1,), (1,)), ((), ()))
NN = (((1,), (0,)), ((), ()))
TN = (((0,), (0,)), ((), ()))


def mm(a, b, dims):
    return lax.dot_general(a, b, dims, preferred_element_type=F32)


def aligned(start, size, unit):
    return pl.ds(pl.multiple_of(start, unit), size)


def lanes_of(products):
    part = products[:, 0:HD]
    for k in range(1, products.shape[1] // HD):
        part = part + products[:, k * HD : (k + 1) * HD]
    return jnp.sum(part.T, axis=0, keepdims=True)


def column_of(row):
    return jnp.broadcast_to(row, (HD, HD)).T


def kernel(
    sizes,
    vq_h, ak_h, av_h, aq_h, vk_h, vv_h, up_h, ao_h, gains, vlen, alen,
    vo_h, aco_h, vqg_h, akg_h, avg_h, aqg_h, vkg_h, vvg_h, gg,
    g, raw_v, raw_a, qn, kn, dvid, vout, vvg, part, rr, rl, xs, xr, fin,
    dka, dva, pb, dpb, mloc, bias_a, bias_v, rbv, rba, small, ssum, sloc, sin, sres, sall,
    gbuf, dbuf, outa,
    ld, gs, gr, ts, tr, s1s, s1r, s2s, s2r, ggs, ggr, ds_, dr_, rs_s, rs_r, ost,
):
    n_tower, n_seq, n_dp = sizes
    n_z = n_seq // 2
    nr = n_z // 2
    nl = n_z - 1 - nr
    heads = 3
    width = heads * HD
    vrows = 512
    arows = n_seq * 64
    depth = n_tower * width
    scale = 1.0 / math.sqrt(HD)
    c = scale * math.log2(math.e)

    t_at = lax.axis_index("tower")
    s_at = lax.axis_index("seq")
    d_at = lax.axis_index("dp")
    z = lax.rem(s_at, n_z)
    x = s_at // n_z

    def seq_id(xx, zz):
        return xx * n_z + zz

    right = seq_id(x, lax.rem(z + 1, n_z))
    left = seq_id(x, lax.rem(z + n_z - 1, n_z))
    over = seq_id(1 - x, z)

    def remote(src, dst, send, recv, **dev):
        return pltpu.make_async_remote_copy(
            src_ref=src, dst_ref=dst, send_sem=send, recv_sem=recv,
            device_id=dev, device_id_type=pl.DeviceIdType.MESH,
        )

    pending = []

    loads = {}
    for n, (src, dst) in enumerate([
        (ao_h, g.at[0, aligned(z * 128 + x * 64, 64, 64)]),
        (av_h, g.at[1, aligned(z * 128 + x * 64, 64, 64)]),
        (aq_h, raw_a.at[0]),
        (ak_h, raw_a.at[1]),
        (vq_h, raw_v.at[0]),
        (vk_h, raw_v.at[1]),
        (vv_h, raw_v.at[2]),
        (up_h, raw_v.at[3]),
    ]):
        loads[n] = pltpu.make_async_copy(src, dst, ld.at[n])
        loads[n].start()

    barrier = pltpu.get_barrier_semaphore()
    peers = 0
    for k in range(1, n_seq):
        pl.semaphore_signal(barrier, inc=1, device_id={"seq": lax.rem(s_at + k, n_seq)}, device_id_type=pl.DeviceIdType.MESH)
        peers += 1
    for k in range(1, n_tower):
        pl.semaphore_signal(barrier, inc=1, device_id={"tower": lax.rem(t_at + k, n_tower)}, device_id_type=pl.DeviceIdType.MESH)
        peers += 1
    if n_dp > 1:
        pl.semaphore_signal(barrier, inc=1, device_id={"dp": 1 - d_at}, device_id_type=pl.DeviceIdType.MESH)
        peers += 1
    pl.semaphore_wait(barrier, peers)

    own = aligned(z * 128 + x * 64, 64, 64)

    def pair(zz):
        return aligned(lax.rem(zz + 2 * n_z, n_z) * 128, 128, 128)

    def gather_x(a):
        copy = remote(g.at[a, own], g.at[a, own], gs.at[a, 0], gr.at[a, 0], seq=over)
        copy.start()
        pending.append(copy)
        return copy

    chains = {}

    def gather_step(a, k):
        mirrored = a % 2 == 1
        long_to, short_to = (left, right) if mirrored else (right, left)
        sign = 1 if mirrored else -1
        if k < nr:
            if k > 0:
                chains[a, "l", k - 1].wait_recv()
            block = g.at[a, pair(z + sign * k)]
            copy = remote(block, block, gs.at[a, 1 + k], gr.at[a, 1 + k], seq=long_to)
            copy.start()
            pending.append(copy)
            chains[a, "l", k] = copy
        if k < nl:
            if k > 0:
                chains[a, "s", k - 1].wait_recv()
            block = g.at[a, pair(z - sign * k)]
            copy = remote(block, block, gs.at[a, 1 + nr + k], gr.at[a, 1 + nr + k], seq=short_to)
            copy.start()
            pending.append(copy)
            chains[a, "s", k] = copy

    def gather_end(a):
        chains[a, "l", nr - 1].wait_recv()
        if nl > 0:
            chains[a, "s", nl - 1].wait_recv()

    loads[0].wait()
    loads[1].wait()
    xc = {0: gather_x(0), 1: gather_x(1)}

    def tower_start(n):
        copies = []
        for k in range(1, n_tower):
            copy = remote(
                small.at[n, t_at], small.at[n, t_at], ts.at[n, k], tr.at[n, k],
                tower=lax.rem(t_at + k, n_tower),
            )
            copy.start()
            pending.append(copy)
            copies.append(copy)
        return copies

    def tower_sum(n, copies):
        for copy in copies:
            copy.wait_recv()
        total = small[n, 0]
        for k in range(1, n_tower):
            total = total + small[n, k]
        return total

    def put_video(n, which, row):
        for k in range(4):
            small[n, t_at, which * 4 + k : which * 4 + k + 1, :] = row[:, k * HD : (k + 1) * HD]

    loads[2].wait()
    loads[3].wait()
    small[0, t_at] = jnp.zeros((16, HD), F32)
    small[1, t_at] = jnp.zeros((16, HD), F32)
    small[2, t_at] = jnp.zeros((16, HD), F32)
    both = jnp.concatenate([raw_a[0].astype(F32), raw_a[1].astype(F32)], axis=0)
    small[0, t_at, 8:9, :] = lanes_of(both * both)
    for n in range(2):
        loads[4 + n].wait()
        wide = raw_v[n].astype(F32)
        put_video(0, n, lanes_of(wide * wide))
    exch = tower_start(0)

    for a in (0, 1):
        xc[a].wait_recv()
        gather_step(a, 0)

    rho = lax.broadcasted_iota(jnp.int32, (arows, HD), 0)
    token = ((rho // 64) % 2) * (n_z * 64) + (rho // 128) * 64 + rho % 64
    bias_a[...] = jnp.where(token < alen[0], 0.0, MASKED)
    vtok = s_at * vrows + lax.broadcasted_iota(jnp.int32, (vrows, HD), 0)
    bias_v[...] = jnp.where(vtok < vlen[0], 0.0, MASKED)

    factors = lax.rsqrt(tower_sum(0, exch) / depth + EPS)
    rba[...] = column_of(factors[8:9, :])
    for n in range(2):
        for h in range(heads):
            cols = slice(h * HD, (h + 1) * HD)
            normed = raw_a[n, :, cols].astype(F32) * rba[n * 64 : n * 64 + 64, :] * gains[2 - n : 3 - n, cols]
            g[2 + n, own, cols] = normed.astype(BF16)
        xc[2 + n] = gather_x(2 + n)
    for n in range(2):
        for k in range(4):
            rows = slice(k * HD, (k + 1) * HD)
            col = column_of(factors[n * 4 + k : n * 4 + k + 1, :])
            rbv[n, rows, :] = col
            for h in range(heads):
                cols = slice(h * HD, (h + 1) * HD)
                normed = raw_v[n, rows, cols].astype(F32) * col * gains[3 * n : 3 * n + 1, cols]
                (qn, kn)[n][rows, cols] = normed.astype(BF16)
    loads[6].wait()
    loads[7].wait()

    for k in range(1, nr):
        for a in (0, 1):
            gather_step(a, k)
        if k == 1:
            for a in (2, 3):
                xc[a].wait_recv()
                gather_step(a, 0)
    if nr == 1:
        for a in (2, 3):
            xc[a].wait_recv()
            gather_step(a, 0)
    for a in (0, 1):
        gather_end(a)
    for k in range(1, nr):
        for a in (2, 3):
            gather_step(a, k)
    for a in (2, 3):
        gather_end(a)

    tile = 256
    tiles = arows // tile
    twice = lambda b: jnp.concatenate([b, b], axis=1)

    def first(i, carry):
        h = i // tiles
        t = lax.rem(i, tiles)
        cols = aligned(h * HD, HD, HD)
        rows = aligned(t * tile, tile, tile)
        s = mm(kn[:, cols], g[2, rows, cols], NT) + twice(bias_v[...])
        m = jnp.maximum(jnp.max(s, axis=0, keepdims=True), FLOOR)
        p = jnp.exp2((s - m) * c)
        dp = mm(raw_v[2, :, cols], g[0, rows, cols], NT)
        total = jnp.sum(p, axis=0, keepdims=True)
        inner = jnp.sum(p * dp, axis=0, keepdims=True)
        pb[h, :, rows] = p.astype(BF16)
        dpb[h, :, rows] = dp
        for k in range(2):
            lanes = slice(k * HD, (k + 1) * HD)
            sloc[t * 2 + k, pl.ds(h, 1), :] = m[:, lanes]
            sloc[t * 2 + k, pl.ds(3 + h, 1), :] = total[:, lanes]
            sloc[t * 2 + k, pl.ds(6 + h, 1), :] = inner[:, lanes]
        return carry

    sloc[...] = jnp.zeros_like(sloc)
    lax.fori_loop(0, heads * tiles, first, 0)

    stat1 = []
    for k in range(1, n_seq):
        to = lax.rem(s_at + k, n_seq)
        copy = remote(sloc.at[lax.rem(to, n_z)], sin.at[s_at], s1s.at[k], s1r.at[k], seq=to)
        copy.start()
        pending.append(copy)
        stat1.append(copy)
    sin[s_at] = sloc[z]

    vtile = 256

    def video_head(h):
        cols = slice(h * HD, (h + 1) * HD)

        def one(t, carry):
            rows = aligned(t * vtile, vtile, vtile)
            q_t = qn[rows, cols]
            u_t = raw_v[3, rows, cols]
            s = mm(g[3, :, cols], q_t, NT) + twice(bias_a[...])
            m = jnp.max(s, axis=0, keepdims=True)
            p = jnp.exp2((s - m) * c)
            w = p * (1.0 / jnp.sum(p, axis=0, keepdims=True))
            low = w.astype(BF16)
            out = mm(g[1, :, cols], low, TN).T.astype(BF16)
            vout[rows, cols] = out
            delta = lanes_of(out.astype(F32) * u_t.astype(F32))
            dp = mm(g[1, :, cols], u_t, NT)
            ds = (w * (dp - delta)).astype(BF16)
            dvid[0, rows, cols] = mm(g[3, :, cols], ds, TN).T * scale
            dka[...] += mm(ds, q_t, NN) * scale
            dva[...] += mm(low, u_t, NN)
            return carry

        dka[...] = jnp.zeros_like(dka)
        dva[...] = jnp.zeros_like(dva)
        lax.fori_loop(0, vrows // vtile, one, 0)
        grad = dka[...]
        gbuf[s_at, 1:2, cols] = jnp.sum(grad * g[3, :, cols].astype(F32), axis=0, keepdims=True) / gains[1:2, cols]
        part[0, :, cols] = grad.astype(BF16)
        part[0, :, width + h * HD : width + (h + 1) * HD] = dva[...].astype(BF16)

    video_head(0)

    for copy in stat1:
        copy.wait_recv()
    mx = sin[0, 0:3, :]
    for k in range(1, n_seq):
        mx = jnp.maximum(mx, sin[k, 0:3, :])
    tot = jnp.zeros((3, HD), F32)
    inn = jnp.zeros((3, HD), F32)
    for k in range(n_seq):
        f = jnp.exp2((sin[k, 0:3, :] - mx) * c)
        tot = tot + sin[k, 3:6, :] * f
        inn = inn + sin[k, 6:9, :] * f
    sres[...] = jnp.zeros_like(sres)
    sres[0:3, :] = mx * c + jnp.log2(tot)
    sres[3:6, :] = inn / tot
    stat2 = []
    for k in range(1, n_z):
        copy = remote(sres, sall.at[z], s2s.at[k], s2r.at[k], seq=seq_id(x, lax.rem(z + k, n_z)))
        copy.start()
        pending.append(copy)
        stat2.append(copy)
    sall[z] = sres[...]

    for h in range(1, heads):
        video_head(h)

    rchain = {}

    def rs_step(b, k):
        for name, n, to, sign, base, land in (("r", nr, right, 1, 0, rr), ("l", nl, left, -1, nr, rl)):
            if k < n:
                block = pair(z + sign * (n - k))
                if k > 0:
                    rchain[b, name, k - 1].wait_recv()
                    part[b, block, :] = (part[b, block, :].astype(F32) + land[b, k - 1].astype(F32)).astype(BF16)
                copy = remote(part.at[b, block], land.at[b, k], rs_s.at[b, base + k], rs_r.at[b, base + k], seq=to)
                copy.start()
                pending.append(copy)
                rchain[b, name, k] = copy

    def rs_cross(b):
        total = part[b, pair(z), :].astype(F32)
        rchain[b, "r", nr - 1].wait_recv()
        total = total + rr[b, nr - 1].astype(F32)
        if nl > 0:
            rchain[b, "l", nl - 1].wait_recv()
            total = total + rl[b, nl - 1].astype(F32)
        fin[b] = total
        xs[b] = fin[b, aligned((1 - x) * 64, 64, 64), :].astype(BF16)
        copy = remote(xs.at[b], xr.at[b], rs_s.at[b, nr + nl], rs_r.at[b, nr + nl], seq=over)
        copy.start()
        pending.append(copy)
        return copy

    def rs_end(b, copy):
        copy.wait_recv()
        return fin[b, aligned(x * 64, 64, 64), :] + xr[b].astype(F32)

    rs_step(0, 0)

    for copy in stat2:
        copy.wait_recv()

    def second_head(h):
        cols = slice(h * HD, (h + 1) * HD)

        def one(t, carry):
            rows = aligned(t * tile, tile, tile)

            def stat(ref, at):
                return jnp.concatenate([ref[t * 2, at : at + 1, :], ref[t * 2 + 1, at : at + 1, :]], axis=1)

            coef = jnp.exp2(stat(sloc, h) * c - stat(sall, h))
            delta = stat(sall, 3 + h)
            w = pb[h, :, rows].astype(F32) * coef
            low = w.astype(BF16)
            out = mm(raw_v[2, :, cols], low, TN).T
            part[1, rows, cols] = out.astype(BF16)
            ds = (w * (dpb[h, :, rows] - delta)).astype(BF16)
            dq = mm(kn[:, cols], ds, TN).T * scale
            q_t = g[2, rows, cols]
            gbuf[s_at, 2:3, cols] += jnp.sum(dq * q_t.astype(F32), axis=0, keepdims=True) / gains[2:3, cols]
            part[1, rows, width + h * HD : width + (h + 1) * HD] = dq.astype(BF16)
            dvid[1, :, cols] += mm(ds, q_t, NN) * scale
            dva[0:vrows, :] += mm(low, g[0, rows, cols], NN)
            return carry

        gbuf[s_at, 2:3, cols] = jnp.zeros((1, HD), F32)
        dvid[1, :, cols] = jnp.zeros((vrows, HD), F32)
        dva[0:vrows, :] = jnp.zeros((vrows, HD), F32)
        lax.fori_loop(0, tiles, one, 0)
        vvg[:, cols] = dva[0:vrows, :].astype(BF16)

    for h in range(heads):
        second_head(h)
        rs_step(0, 1 + h)
    rs_step(1, 0)

    for n, row in ((0, 0), (1, 3)):
        inner = dvid[n] * (qn, kn)[n][...].astype(F32)
        put_video(1, n, lanes_of(inner))
        gbuf[s_at, row : row + 1, :] = jnp.sum(inner, axis=0, keepdims=True) / gains[row : row + 1, :]
    exch = tower_start(1)
    gcopies = []
    for k in range(1, n_seq):
        copy = remote(gbuf.at[s_at], gbuf.at[s_at], ggs.at[k], ggr.at[k], seq=lax.rem(s_at + k, n_seq))
        copy.start()
        pending.append(copy)
        gcopies.append(copy)
    rs_step(1, 1)
    cross0 = rs_cross(0)
    outs = [
        pltpu.make_async_copy(vout, vo_h, ost.at[0]),
        pltpu.make_async_copy(vvg, vvg_h, ost.at[1]),
    ]
    for copy in outs:
        copy.start()

    inner = tower_sum(1, exch) * (1.0 / depth)
    for n in range(2):
        row = 3 * n
        for k in range(4):
            rows = slice(k * HD, (k + 1) * HD)
            col = column_of(inner[n * 4 + k : n * 4 + k + 1, :])
            r = rbv[n, rows, :]
            for h in range(heads):
                cols = slice(h * HD, (h + 1) * HD)
                grad = r * gains[row : row + 1, cols] * dvid[n, rows, cols] - raw_v[n, rows, cols].astype(F32) * (r * r * col)
                (qn, kn)[n][rows, cols] = grad.astype(BF16)
        copy = pltpu.make_async_copy((qn, kn)[n], (vqg_h, vkg_h)[n], ost.at[2 + n])
        copy.start()
        outs.append(copy)
    rs_step(1, 2)

    for copy in gcopies:
        copy.wait_recv()
    total = gbuf[0, 0:4, :]
    for k in range(1, n_seq):
        total = total + gbuf[k, 0:4, :]
    if n_dp > 1:
        dbuf[d_at, 0:4, :] = total
        copy = remote(dbuf.at[d_at], dbuf.at[d_at], ds_.at[0], dr_.at[0], dp=1 - d_at)
        copy.start()
        pending.append(copy)

    key_side = rs_end(0, cross0)
    rs_step(1, 3)
    outa[3] = key_side[:, width:].astype(BF16)
    if n_dp > 1:
        copy.wait_recv()
        gg[...] = dbuf[0, 0:4, :] + dbuf[1, 0:4, :]
    else:
        gg[...] = total
    cross1 = rs_cross(1)
    query_side = rs_end(1, cross1)
    outa[0] = query_side[:, 0:width].astype(BF16)
    sides = (query_side[:, width:], key_side[:, 0:width])
    inner = jnp.concatenate([sides[n] * g[2 + n, own, :].astype(F32) for n in range(2)], axis=0)
    small[2, t_at, 0:1, :] = lanes_of(inner)
    exch = tower_start(2)
    col = column_of(tower_sum(2, exch)[0:1, :] * (1.0 / depth))
    for n in range(2):
        half = slice(n * 64, n * 64 + 64)
        r = rba[half, :]
        for h in range(heads):
            cols = slice(h * HD, (h + 1) * HD)
            grad = r * gains[2 - n : 3 - n, cols] * sides[n][:, cols] - raw_a[n, :, cols].astype(F32) * (r * r * col[half, :])
            outa[1 + n, :, cols] = grad.astype(BF16)
    for n, dst in enumerate((aco_h, aqg_h, akg_h, avg_h)):
        copy = pltpu.make_async_copy(outa.at[n], dst, ost.at[4 + n])
        copy.start()
        outs.append(copy)
    for copy in outs:
        copy.wait()
    for copy in pending:
        copy.wait_send()


def solution(mesh):
    sizes = tuple(mesh.shape[name] for name in ("tower", "seq", "dp"))
    n_tower, n_seq, n_dp = sizes
    n_z = n_seq // 2
    arows = n_seq * 64
    hops = n_z - 1
    nr = n_z // 2
    nl = max(hops - nr, 1)
    width = 384
    any_spec = pl.BlockSpec(memory_space=pl.ANY)
    vmem = pl.BlockSpec(memory_space=pltpu.VMEM)
    smem = pl.BlockSpec(memory_space=pltpu.SMEM)
    dma = lambda *shape: pltpu.SemaphoreType.DMA(shape)

    def body(vq, ak, av, aq, vk, vv, up, ao, gains, vlen, alen):
        video = jax.ShapeDtypeStruct((512, width), BF16)
        audio = jax.ShapeDtypeStruct((64, width), BF16)
        results = pl.pallas_call(
            functools.partial(kernel, sizes),
            out_shape=(video, audio, video, audio, audio, audio, video, video, jax.ShapeDtypeStruct((4, width), F32)),
            in_specs=[any_spec] * 8 + [vmem, smem, smem],
            out_specs=tuple([any_spec] * 8 + [vmem]),
            scratch_shapes=[
                pltpu.VMEM((4, arows, width), BF16),
                pltpu.VMEM((4, 512, width), BF16),
                pltpu.VMEM((2, 64, width), BF16),
                pltpu.VMEM((512, width), BF16),
                pltpu.VMEM((512, width), BF16),
                pltpu.VMEM((2, 512, width), F32),
                pltpu.VMEM((512, width), BF16),
                pltpu.VMEM((512, width), BF16),
                pltpu.VMEM((2, arows, 2 * width), BF16),
                pltpu.VMEM((2, nr, 128, 2 * width), BF16),
                pltpu.VMEM((2, nl, 128, 2 * width), BF16),
                pltpu.VMEM((2, 64, 2 * width), BF16),
                pltpu.VMEM((2, 64, 2 * width), BF16),
                pltpu.VMEM((2, 128, 2 * width), F32),
                pltpu.VMEM((max(arows, 512), HD), F32),
                pltpu.VMEM((max(arows, 512), HD), F32),
                pltpu.VMEM((3, 512, arows), BF16),
                pltpu.VMEM((3, 512, arows), F32),
                pltpu.VMEM((8, HD), F32),
                pltpu.VMEM((arows, HD), F32),
                pltpu.VMEM((512, HD), F32),
                pltpu.VMEM((2, 512, HD), F32),
                pltpu.VMEM((128, HD), F32),
                pltpu.VMEM((3, n_tower, 16, HD), F32),
                pltpu.VMEM((16, HD), F32),
                pltpu.VMEM((n_z, 16, HD), F32),
                pltpu.VMEM((n_seq, 16, HD), F32),
                pltpu.VMEM((8, HD), F32),
                pltpu.VMEM((n_z, 8, HD), F32),
                pltpu.VMEM((n_seq, 8, width), F32),
                pltpu.VMEM((2, 8, width), F32),
                pltpu.VMEM((4, 64, width), BF16),
                dma(8), dma(4, hops + 1), dma(4, hops + 1), dma(3, n_tower), dma(3, n_tower),
                dma(n_seq), dma(n_seq), dma(n_z), dma(n_z), dma(n_seq), dma(n_seq), dma(1), dma(1),
                dma(2, hops + 1), dma(2, hops + 1), dma(8),
            ],
            compiler_params=pltpu.CompilerParams(
                collective_id=0, has_side_effects=True, vmem_limit_bytes=56 * 1024 * 1024
            ),
            cost_estimate=pl.CostEstimate(flops=4_800_000_000, bytes_accessed=4_000_000, transcendentals=3_200_000),
        )(vq[0], ak[0], av[0], aq[0], vk[0], vv[0], up[0], ao[0], gains, vlen, alen)
        return tuple(r[None] for r in results[:8]) + (results[8],)

    spec = P("dp", "seq", "tower")
    return jax.shard_map(
        body,
        mesh=mesh,
        in_specs=(spec,) * 8 + (P(None, "tower"), P("dp"), P("dp")),
        out_specs=(spec,) * 8 + (P(None, "tower"),),
        check_vma=False,
    )
```

time: 582 us -> 138 us (0.24)
  blocking collectives: 391 us -> 0 us
  Pallas kernels: 0 us -> 127 us
  other arithmetic: 46 us -> 0 us
  waiting for transfers between devices: 43.1 us -> 0 us
  local copies, waits for them, and re-layouts: 46.9 us -> 7.99 us
  matrix products: 32.6 us -> 0 us
  between operations: 15.7 us -> 1.97 us
    all_gather x6 -> x0, blocking collectives: 215 us -> none  [the longest x2 64.1 us: combined_all(): everything = jax.tree.map(lambda part: lax.all_gather(part, axis), value)]
    psum x4 -> x0, blocking collectives: 176 us -> none  [the longest x1 75.4 us: body(): whole_output = lax.psum(part_output, 'seq').astype(jnp.bfloat16)]
    pallas_call x0 -> x1, Pallas kernels: none -> 127 us  [body(): pl.pallas_call(functools.partial(kernel, sizes), out_shape=(video, audio,...]
    unnamed x5 -> x0, waiting for transfers between devices: 43.1 us -> none
    dot_general x12 -> x0, matrix products: 32.6 us -> none  [the longest x1 5.71 us: body(): jnp.einsum('opfb,otfb->ofpt', agrad_heads, vvalue_heads, preferred_elemen...]
    unnamed x107 -> x25, local copies, waits for them, and re-layouts: 34.3 us -> 7.99 us
    add x16 -> x0, other arithmetic: 20.5 us -> none  [the longest x15 20.5 us: combine_partial(): former[1] * jnp.exp(former[0] - largest)]
    convert_element_type x7 -> x0, other arithmetic: 10 us -> none  [the longest x1 4.51 us: body(): aweights_low = aweights.astype(jnp.bfloat16)]
  transfers between devices with their start and end apart: 3 -> 0, of which waited for: 1 -> 0; matrix products, arithmetic and copies ran while one was open for 16% -> 0% of each run, Pallas kernels for 0% -> 0%
where the time goes in v1:
time: 138 us; the launch traced here: 136 us
  Pallas kernels  127 us (92%)
  local copies, waits for them, and re-layouts  7.99 us (6%)
  between operations  1.97 us (1%)
    pallas_call x1, Pallas kernels, body(): pl.pallas_call(functools.partial(kernel, sizes), out_shape=(video, audio,...  127 us
    unnamed x25, local copies, waits for them, and re-layouts  7.99 us

profile of v1, /device:TPU:8, one launch (start us, length us, event | category | flops | bytes accessed | tf_op | source)
XLA Modules:
  0.0 136.5 jit_solution(9990765268553321967)
XLA Ops:
  1.9 126.5 %shard_map.178 = (bf16[512,384]{1,0:T(8,128)(2,1)}, bf16[64,384]{1,0:T(8,128)(2,1)}, bf16[512,384]{1,0:T(8,128)(2,1)}, bf16[64,384]{1,0:T(8,128)(2,1)}, bf16[64,...) custom-call(bf16[512,384]{1,0:T(8,128)(2,1)} %bitcast.24, ...), custom_call_target="tpu_custom_call" | custom-call | flops 4800000000 | bytes 4000000 | tf_op jit(solution)/shard_map/pallas_call | solution.py:504
  128.5 0.0 copy-start.6
  128.5 0.0 copy-start.2
  128.5 1.8 %copy.31 = bf16[1,512,384]{2,1,0:T(8,128)(2,1)} copy(bf16[1,512,384]{2,1,0:T(8,128)(2,1)} %bitcast.19) | data formatting | bytes 786432
  130.3 0.0 copy-done.6
  130.3 0.6 copy.32
  130.9 0.0 copy-done.2
  130.9 0.0 copy-start.5
  130.9 0.7 copy.33
  131.7 0.0 copy-done.5
  131.7 0.0 copy-start.4
  131.7 0.6 copy.34
  132.4 0.2 copy-done.4
  132.5 0.0 copy-start.3
  132.5 0.6 copy.35
  133.2 0.2 copy-done.3
  133.4 0.6 copy.36
  134.0 0.0 copy-done.1
  134.0 0.0 copy-start
  134.0 0.7 copy.37
  134.7 0.4 copy-done
  135.1 0.7 copy.38
  135.9 0.0 copy-done.7
  135.9 0.6 copy.39
  (2 shorter events, 0.0 us)
Async XLA Ops:
  128.5 1.9 %copy-start.6 = (bf16[64,384]{1,0:T(8,128)(2,1)S(1)}, bf16[64,384]{1,0:T(8,128)(2,1)}, u32[]{:S(2)}) copy-start(bf16[64,384]{1,0:T(8,128)(2,1)} %get-tuple-element.19) | copy-start | bytes 147460
  128.5 2.5 %copy-start.2 = (bf16[512,384]{1,0:T(8,128)(2,1)S(1)}, bf16[512,384]{1,0:T(8,128)(2,1)}, u32[]{:S(2)}) copy-start(bf16[512,384]{1,0:T(8,128)(2,1)} %get-tuple-element.20) | copy-start | bytes 1179652
  130.9 0.8 copy-start.5
  130.9 3.1 %copy-start.1 = (bf16[512,384]{1,0:T(8,128)(2,1)S(1)}, bf16[512,384]{1,0:T(8,128)(2,1)}, u32[]{:S(2)}) copy-start(bf16[512,384]{1,0:T(8,128)(2,1)} %get-tuple-element.24) | copy-start | bytes 1179652
  131.7 0.8 copy-start.4
  132.5 0.8 copy-start.3
  134.0 1.1 copy-start
  135.1 0.8 copy-start.7

commit v2 on v1

v2 whole, which is shorter than its diff:
```python
import functools
import math

import jax
import jax.numpy as jnp
from jax import lax
from jax.experimental import pallas as pl
from jax.experimental.pallas import tpu as pltpu
from jax.sharding import PartitionSpec as P

HD = 128
HEADS = 3
WIDTH = HEADS * HD
VROWS = 512
EPS = 1e-06
MASKED = -1e30
FLOOR = -1e29
F32 = jnp.float32
BF16 = jnp.bfloat16
MESH = pl.DeviceIdType.MESH

NT = (((1,), (1,)), ((), ()))
NN = (((1,), (0,)), ((), ()))
TN = (((0,), (0,)), ((), ()))


def mm(a, b, dims):
    return lax.dot_general(a, b, dims, preferred_element_type=F32)


def aligned(start, size, unit):
    return pl.ds(pl.multiple_of(start, unit), size)


def lanes_of(products):
    part = products[:, 0:HD]
    for k in range(1, products.shape[1] // HD):
        part = part + products[:, k * HD : (k + 1) * HD]
    return jnp.sum(part.T, axis=0, keepdims=True)


def column_of(row):
    return jnp.broadcast_to(row, (HD, HD)).T


def head_cols(h):
    return slice(h * HD, (h + 1) * HD)


def wide(block, n):
    return jnp.concatenate([block] * n, axis=1)


def kernel(
    sizes,
    vq_h, ak_h, av_h, aq_h, vk_h, vv_h, up_h, ao_h, gains, vlen, alen,
    vo_h, aco_h, vqg_h, akg_h, avg_h, aqg_h, vkg_h, vvg_h, gg_h,
    g, raw_v, raw_a, qn, kn, dvid, vout, vvg, part, rr, rl, xin, xs, xr, fin,
    pa, dpa, dsa, ast, acf, pb, dpb, dsb, acc, bias_a, bias_v, rbv, rba, small,
    sloc, sin, sres, sall, ub, uin, ucol, gbuf, dbuf, gout, outa,
    ld, gs, gr, gxs, gxr, ts, tr, s1s, s1r, s2s, s2r, us, ur, ggs, ggr, ds_, dr_,
    rs_s, rs_r, xi_s, xi_r, ost,
):
    n_tower, n_seq, n_dp = sizes
    n_z = n_seq // 2
    nr = n_z // 2
    nl = n_z - 1 - nr
    arows = n_seq * 64
    depth = n_tower * WIDTH
    scale = 1.0 / math.sqrt(HD)
    c = scale * math.log2(math.e)
    unscale = scale / c

    t_at = lax.axis_index("tower")
    s_at = lax.axis_index("seq")
    d_at = lax.axis_index("dp")
    z = lax.rem(s_at, n_z)
    x = s_at // n_z

    def ring(zz):
        return lax.rem(zz + 2 * n_z, n_z)

    def seq_id(xx, zz):
        return xx * n_z + ring(zz)

    right, left, over = seq_id(x, z + 1), seq_id(x, z - 1), seq_id(1 - x, z)

    pending = []

    def send(src, dst, send_sem, recv_sem, **dev):
        copy = pltpu.make_async_remote_copy(
            src_ref=src, dst_ref=dst, send_sem=send_sem, recv_sem=recv_sem,
            device_id=dev, device_id_type=MESH,
        )
        copy.start()
        pending.append(copy)
        return copy

    own = aligned(z * 128 + x * 64, 64, 64)
    loads = []
    for n, (src, dst) in enumerate([
        (aq_h, raw_a.at[0]),
        (ak_h, raw_a.at[1]),
        (ao_h, g.at[0, own]),
        (av_h, g.at[1, own]),
        (vq_h, raw_v.at[0]),
        (vk_h, raw_v.at[1]),
        (vv_h, raw_v.at[2]),
        (up_h, raw_v.at[3]),
    ]):
        loads.append(pltpu.make_async_copy(src, dst, ld.at[n]))
        loads[n].start()
    barrier = pltpu.get_barrier_semaphore()
    peers = 0
    for k in range(1, n_seq):
        pl.semaphore_signal(barrier, inc=1, device_id={"seq": lax.rem(s_at + k, n_seq)}, device_id_type=MESH)
        peers += 1
    for k in range(1, n_tower):
        pl.semaphore_signal(barrier, inc=1, device_id={"tower": lax.rem(t_at + k, n_tower)}, device_id_type=MESH)
        peers += 1
    if n_dp > 1:
        pl.semaphore_signal(barrier, inc=1, device_id={"dp": 1 - d_at}, device_id_type=MESH)
        peers += 1

    def put_video(n, which, row):
        for k in range(4):
            small[n, t_at, which * 4 + k : which * 4 + k + 1, :] = row[:, k * HD : (k + 1) * HD]

    for n in range(3):
        small[n, t_at] = jnp.zeros((16, HD), F32)
    sloc[...] = jnp.zeros_like(sloc)
    sres[...] = jnp.zeros_like(sres)
    ub[...] = jnp.zeros_like(ub)
    gbuf[s_at] = jnp.zeros((8, WIDTH), F32)
    loads[0].wait()
    loads[1].wait()
    both = jnp.concatenate([raw_a[0].astype(F32), raw_a[1].astype(F32)], axis=0)
    small[0, t_at, 8:9, :] = lanes_of(both * both)
    rho = lax.broadcasted_iota(jnp.int32, (arows, HD), 0)
    token = ((rho // 64) % 2) * (n_z * 64) + (rho // 128) * 64 + rho % 64
    bias_a[...] = jnp.where(token < alen[0], 0.0, MASKED)
    vtok = s_at * VROWS + lax.broadcasted_iota(jnp.int32, (VROWS, HD), 0)
    bias_v[...] = jnp.where(vtok < vlen[0], 0.0, MASKED)
    for n in range(2):
        loads[4 + n].wait()
        widened = raw_v[n].astype(F32)
        put_video(0, n, lanes_of(widened * widened))
    for n in (2, 3, 6, 7):
        loads[n].wait()
    pl.semaphore_wait(barrier, peers)

    def tower_start(n):
        return [
            send(small.at[n, t_at], small.at[n, t_at], ts.at[n, k], tr.at[n, k], tower=lax.rem(t_at + k, n_tower))
            for k in range(1, n_tower)
        ]

    def tower_sum(n, copies):
        for copy in copies:
            copy.wait_recv()
        total = small[n, 0]
        for k in range(1, n_tower):
            total = total + small[n, k]
        return total

    chains = {}

    def gather_step(a, k):
        last_over = a % 2 == 0
        sign = 1 if a >= 2 else -1
        ways = (("l", nr, left if a >= 2 else right, sign, 0), ("s", nl, right if a >= 2 else left, -sign, nr))

        def block(zz):
            if last_over:
                return g.at[a, aligned(ring(zz) * 128 + x * 64, 64, 64)]
            return g.at[a, aligned(ring(zz) * 128, 128, 128)]

        if k == 0 and last_over:
            chains[a, "x", 0] = send(block(z), block(z), gxs.at[a // 2, 0], gxr.at[a // 2, 0], seq=over)
        for name, n, to, way, base in ways:
            if k > n:
                continue
            here = block(z + way * k)
            if k > 0:
                chains[a, name, k].wait_recv()
            if k < n:
                chains[a, name, k + 1] = send(here, here, gs.at[a, 1 + base + k], gr.at[a, 1 + base + k], seq=to)
            if k > 0 and last_over:
                chains[a, "x", base + k] = send(here, here, gxs.at[a // 2, base + k], gxr.at[a // 2, base + k], seq=over)

    def gather_over(a):
        chains[a, "x", 0] = send(g.at[a, own], g.at[a, own], gs.at[a, 0], gr.at[a, 0], seq=over)

    def over_wait(a, delta):
        towards = delta if a >= 2 else -delta
        if delta == 0:
            at = 0
        elif abs(delta) == nr or towards > 0:
            at = abs(delta)
        else:
            at = nr + abs(delta)
        chains[a, "x", at].wait_recv()

    exch = tower_start(0)
    gather_over(1)
    gather_step(0, 0)

    stat1 = []

    def audio_first(delta):
        at = ring(z + delta)
        rows = aligned(at * 128, 128, 128)
        over_wait(0, delta)
        over_wait(2, delta)

        def one(h, carry):
            cols = aligned(h * HD, HD, HD)
            s = mm(kn[:, cols], g[2, rows, cols], NT) + bias_v[...]
            m = jnp.maximum(jnp.max(s, axis=0, keepdims=True), FLOOR)
            p = jnp.exp2(s - m)
            dp = mm(raw_v[2, :, cols], g[0, rows, cols], NT)
            pb[h, :, rows] = p.astype(BF16)
            dpb[h, :, rows] = dp
            sloc[at, pl.ds(h, 1), :] = m
            sloc[at, pl.ds(3 + h, 1), :] = jnp.sum(p, axis=0, keepdims=True)
            sloc[at, pl.ds(6 + h, 1), :] = jnp.sum(p * dp, axis=0, keepdims=True)
            return carry

        lax.fori_loop(0, HEADS, one, 0)
        slot = delta % n_z
        for k, xx in enumerate((x, 1 - x)):
            if delta == 0 and k == 0:
                sin[s_at] = sloc[at]
            else:
                stat1.append(
                    send(sloc.at[at], sin.at[s_at], s1s.at[2 * slot + k], s1r.at[2 * slot + k], seq=seq_id(xx, at))
                )

    def video_first(delta):
        at = ring(z + delta)
        rows = aligned(at * 128, 128, 128)

        def one(h, carry):
            cols = aligned(h * HD, HD, HD)
            s = mm(g[3, rows, cols], qn[:, cols], NT) + wide(bias_a[rows, :], 4)
            m = jnp.maximum(jnp.max(s, axis=0, keepdims=True), FLOOR)
            p = jnp.exp2(s - m)
            dp = mm(g[1, rows, cols], raw_v[3, :, cols], NT)
            pa[h, rows, :] = p.astype(BF16)
            dpa[h, rows, :] = dp
            ast[h, at, 0:1, :] = m
            ast[h, at, 1:2, :] = jnp.sum(p, axis=0, keepdims=True)
            ast[h, at, 2:3, :] = jnp.sum(p * dp, axis=0, keepdims=True)
            return carry

        lax.fori_loop(0, HEADS, one, 0)

    def factor_audio(factors):
        rba[...] = column_of(factors[8:9, :])
        for n in range(2):
            half = slice(n * 64, n * 64 + 64)
            for h in range(HEADS):
                cols = head_cols(h)
                gain = gains[2 - n : 3 - n, cols] * (c if n == 0 else 1.0)
                g[2 + n, own, cols] = (raw_a[n, :, cols].astype(F32) * rba[half, :] * gain).astype(BF16)

    def factor_video(factors):
        for n in range(2):
            for k in range(4):
                rows = slice(k * HD, (k + 1) * HD)
                col = column_of(factors[n * 4 + k : n * 4 + k + 1, :])
                rbv[n, rows, :] = col
                for h in range(HEADS):
                    cols = head_cols(h)
                    gain = gains[3 * n : 3 * n + 1, cols] * (c if n == 0 else 1.0)
                    (qn, kn)[n][rows, cols] = (raw_v[n, rows, cols].astype(F32) * col * gain).astype(BF16)

    chains[1, "x", 0].wait_recv()
    gather_step(1, 0)
    gather_step(0, 1)
    factors = lax.rsqrt(tower_sum(0, exch) / depth + EPS)
    factor_audio(factors)
    gather_step(2, 0)
    gather_over(3)
    factor_video(factors)
    far = nr

    def maybe(a, k):
        if k <= far:
            gather_step(a, k)

    maybe(0, 2)
    maybe(1, 1)
    maybe(2, 1)
    chains[3, "x", 0].wait_recv()
    gather_step(3, 0)
    maybe(0, 3)
    audio_first(0)
    maybe(1, 2)
    maybe(2, 2)
    maybe(3, 1)
    video_first(0)
    maybe(0, 4)
    maybe(1, 3)
    maybe(2, 3)
    maybe(3, 2)

    def both_ways(run, dist):
        run(-dist)
        if dist <= nl:
            run(dist)

    both_ways(audio_first, 1)
    maybe(2, 4)
    maybe(1, 4)
    maybe(3, 3)
    both_ways(video_first, 1)
    for dist in range(2, nr + 1):
        both_ways(audio_first, dist)
        if dist == 2:
            maybe(3, 4)
        both_ways(video_first, dist)

    def video_second(h):
        cols = head_cols(h)
        m = ast[h, 0, 0:1, :]
        for k in range(1, n_z):
            m = jnp.maximum(m, ast[h, k, 0:1, :])
        total = jnp.zeros((1, VROWS), F32)
        inner = jnp.zeros((1, VROWS), F32)
        for k in range(n_z):
            f = jnp.exp2(ast[h, k, 0:1, :] - m)
            acf[k, 0:1, :] = f
            total = total + f * ast[h, k, 1:2, :]
            inner = inner + f * ast[h, k, 2:3, :]
        inverse = 1.0 / total
        delta = inner * inverse

        def one(k, carry):
            rows = aligned(k * 128, 128, 128)
            w = pa[h, rows, :].astype(F32) * (acf[k, 0:1, :] * inverse)
            pa[h, rows, :] = w.astype(BF16)
            dsa[rows, :] = (w * (dpa[h, rows, :] - delta)).astype(BF16)
            return carry

        lax.fori_loop(0, n_z, one, 0)
        low = pa[h]
        ds = dsa[...]
        dk = mm(ds, qn[:, cols], NN) * unscale
        part[0, :, h * 256 : h * 256 + HD] = dk.astype(BF16)
        part[0, :, h * 256 + HD : h * 256 + 256] = mm(low, raw_v[3, :, cols], NN).astype(BF16)
        prod = dk * g[3, :, cols].astype(F32)
        gbuf[s_at, 1:2, cols] = jnp.sum(prod, axis=0, keepdims=True) / gains[1:2, cols]
        acc[0] = prod if h == 0 else acc[0] + prod
        vout[:, cols] = mm(g[1, :, cols], low, TN).T.astype(BF16)
        dvid[0, :, cols] = mm(g[3, :, cols], ds, TN).T * scale

    tile = 256
    tiles = arows // tile

    def audio_second(h):
        cols = head_cols(h)

        def one(t, carry):
            lanes = aligned(t * tile, tile, tile)

            def stat(ref, at):
                return jnp.concatenate([ref[t * 2, at : at + 1, :], ref[t * 2 + 1, at : at + 1, :]], axis=1)

            coef = jnp.exp2(stat(sloc, h) - stat(sall, h))
            delta = stat(sall, 3 + h)
            w = pb[h, :, lanes].astype(F32) * coef
            pb[h, :, lanes] = w.astype(BF16)
            dsb[:, lanes] = (w * (dpb[h, :, lanes] - delta)).astype(BF16)
            return carry

        lax.fori_loop(0, tiles, one, 0)
        low = pb[h]
        ds = dsb[...]
        part[1, :, h * 256 : h * 256 + HD] = mm(raw_v[2, :, cols], low, TN).T.astype(BF16)
        dq = mm(kn[:, cols], ds, TN).T * scale
        part[1, :, h * 256 + HD : h * 256 + 256] = dq.astype(BF16)
        prod = dq * g[2, :, cols].astype(F32) * (1.0 / c)
        gbuf[s_at, 2:3, cols] = jnp.sum(prod, axis=0, keepdims=True) / gains[2:3, cols]
        acc[1] = prod if h == 0 else acc[1] + prod
        dvid[1, :, cols] = mm(ds, g[2, :, cols], NN) * unscale
        vvg[:, cols] = mm(low, g[0, :, cols], NN).astype(BF16)

    rchain = {}

    def group(h):
        return slice(h * 256, (h + 1) * 256)

    def scatter_over(h):
        for k, delta in enumerate(order):
            at = ring(z + delta)
            rchain[h, "x", delta % n_z] = send(
                part.at[1, aligned(at * 128 + (1 - x) * 64, 64, 64), group(h)],
                xin.at[at, :, group(h)],
                xi_s.at[h, k], xi_r.at[h, k], seq=over,
            )

    order = []
    for dist in range(nr, 0, -1):
        order.append(dist)
        if dist <= nl:
            order.append(-dist)
    order.append(0)

    def scatter_step(b, h, k):
        cols = group(h)
        for name, n, to, way, base, land in (("r", nr, right, 1, 0, rr), ("l", nl, left, -1, nr, rl)):
            if k >= n:
                continue
            delta = way * (n - k)
            at = ring(z + delta)
            size = 128 if b == 0 else 64
            rows = aligned(at * 128, 128, 128) if b == 0 else aligned(at * 128 + x * 64, 64, 64)
            if b == 1 or k > 0:
                total = part[b, rows, cols].astype(F32)
                if b == 1:
                    rchain[h, "x", delta % n_z].wait_recv()
                    total = total + xin[at, :, cols].astype(F32)
                if k > 0:
                    rchain[b, h, name, k - 1].wait_recv()
                    total = total + land[b, k - 1, 0:size, cols].astype(F32)
                part[b, rows, cols] = total.astype(BF16)
            rchain[b, h, name, k] = send(
                part.at[b, rows, cols], land.at[b, k, 0:size, cols],
                rs_s.at[b, h, base + k], rs_r.at[b, h, base + k], seq=to,
            )

    def scatter_landed(b, h, total, size):
        cols = group(h)
        rchain[b, h, "r", nr - 1].wait_recv()
        total = total + rr[b, nr - 1, 0:size, cols].astype(F32)
        if nl > 0:
            rchain[b, h, "l", nl - 1].wait_recv()
            total = total + rl[b, nl - 1, 0:size, cols].astype(F32)
        return total

    def key_cross(h):
        cols = group(h)
        fin[:, cols] = scatter_landed(0, h, part[0, aligned(z * 128, 128, 128), cols].astype(F32), 128)
        xs[:, cols] = fin[aligned((1 - x) * 64, 64, 64), cols].astype(BF16)
        rchain[h, "k"] = send(xs.at[:, cols], xr.at[:, cols], rs_s.at[0, h, n_z - 1], rs_r.at[0, h, n_z - 1], seq=over)

    def key_end(h):
        cols = group(h)
        rchain[h, "k"].wait_recv()
        return fin[aligned(x * 64, 64, 64), cols] + xr[:, cols].astype(F32)

    def query_end(h):
        cols = group(h)
        rchain[h, "x", 0].wait_recv()
        return scatter_landed(1, h, part[1, own, cols].astype(F32) + xin[z, :, cols].astype(F32), 64)

    video_second(0)
    scatter_step(0, 0, 0)

    for copy in stat1:
        copy.wait_recv()
    mx = sin[0, 0:3, :]
    for k in range(1, n_seq):
        mx = jnp.maximum(mx, sin[k, 0:3, :])
    tot = jnp.zeros((3, HD), F32)
    inn = jnp.zeros((3, HD), F32)
    for k in range(n_seq):
        f = jnp.exp2(sin[k, 0:3, :] - mx)
        tot = tot + sin[k, 3:6, :] * f
        inn = inn + sin[k, 6:9, :] * f
    sres[0:3, :] = mx + jnp.log2(tot)
    sres[3:6, :] = inn / tot
    stat2 = [send(sres, sall.at[z], s2s.at[k], s2r.at[k], seq=seq_id(x, z + k)) for k in range(1, n_z)]
    sall[z] = sres[...]

    def steps(b, at):
        for h in range(HEADS):
            k = at - h
            if 0 <= k < nr:
                scatter_step(b, h, k)

    video_second(1)
    steps(0, 1)
    video_second(2)
    steps(0, 2)
    for copy in stat2:
        copy.wait_recv()
    audio_second(0)
    scatter_over(0)
    steps(0, 3)
    audio_second(1)
    scatter_over(1)
    steps(0, 4)
    audio_second(2)
    scatter_over(2)
    steps(0, 5)

    for n, row in ((0, 0), (1, 3)):
        inner = dvid[n] * (qn, kn)[n][...].astype(F32) * (1.0 / c if n == 0 else 1.0)
        put_video(1, n, lanes_of(inner))
        gbuf[s_at, row : row + 1, :] = jnp.sum(inner, axis=0, keepdims=True) / gains[row : row + 1, :]
    exch = tower_start(1)
    for n in range(2):
        row = lanes_of(acc[n])
        for k in range(n_z):
            ub[k, n : n + 1, :] = row[:, k * HD : (k + 1) * HD]
    ucopies = []
    for k in range(1, n_seq):
        to = lax.rem(s_at + k, n_seq)
        ucopies.append(send(ub.at[lax.rem(to, n_z)], uin.at[s_at], us.at[k], ur.at[k], seq=to))
    uin[s_at] = ub[z]
    gcopies = [
        send(gbuf.at[s_at], gbuf.at[s_at], ggs.at[k], ggr.at[k], seq=lax.rem(s_at + k, n_seq))
        for k in range(1, n_seq)
    ]
    outs = []

    def write(src, dst):
        copy = pltpu.make_async_copy(src, dst, ost.at[len(outs)])
        copy.start()
        outs.append(copy)

    write(vout, vo_h)
    write(vvg, vvg_h)
    steps(1, 0)
    for h in range(HEADS):
        key_cross(h)
    steps(1, 1)

    inner = tower_sum(1, exch) * (1.0 / depth)

    def video_grad(n):
        row = 3 * n
        for k in range(4):
            rows = slice(k * HD, (k + 1) * HD)
            col = column_of(inner[n * 4 + k : n * 4 + k + 1, :])
            r = rbv[n, rows, :]
            for h in range(HEADS):
                cols = head_cols(h)
                grad = r * gains[row : row + 1, cols] * dvid[n, rows, cols] - raw_v[n, rows, cols].astype(F32) * (r * r * col)
                (qn, kn)[n][rows, cols] = grad.astype(BF16)
        write((qn, kn)[n], (vqg_h, vkg_h)[n])

    video_grad(0)
    steps(1, 2)
    for copy in ucopies:
        copy.wait_recv()
    total = uin[0]
    for k in range(1, n_seq):
        total = total + uin[k]
    small[2, t_at, 0:8, :] = total
    uexch = tower_start(2)
    video_grad(1)
    steps(1, 3)
    for copy in gcopies:
        copy.wait_recv()
    total = gbuf[0]
    for k in range(1, n_seq):
        total = total + gbuf[k]
    if n_dp > 1:
        dbuf[d_at] = total
        gcopy = send(dbuf.at[d_at], dbuf.at[d_at], ds_.at[0], dr_.at[0], dp=1 - d_at)
    steps(1, 4)
    uall = tower_sum(2, uexch) * (1.0 / depth)
    for n in range(2):
        ucol[n] = column_of(uall[n : n + 1, :])

    def audio_grad(n, h, total):
        cols = head_cols(h)
        r = rba[(1 - n) * 64 : (2 - n) * 64, :]
        col = ucol[n, aligned(x * 64, 64, 64), :]
        return (r * gains[n + 1 : n + 2, cols] * total - raw_a[1 - n, :, cols].astype(F32) * (r * r * col)).astype(BF16)

    for h in range(HEADS):
        both = key_end(h)
        outa[2, :, head_cols(h)] = audio_grad(0, h, both[:, 0:HD])
        outa[3, :, head_cols(h)] = both[:, HD:].astype(BF16)
    write(outa.at[2], akg_h)
    write(outa.at[3], avg_h)
    if n_dp > 1:
        gcopy.wait_recv()
        total = dbuf[0] + dbuf[1]
    gout[...] = total[0:4, :]
    write(gout, gg_h)
    steps(1, 5)
    for h in range(HEADS):
        both = query_end(h)
        outa[0, :, head_cols(h)] = both[:, 0:HD].astype(BF16)
        outa[1, :, head_cols(h)] = audio_grad(1, h, both[:, HD:])
    write(outa.at[0], aco_h)
    write(outa.at[1], aqg_h)
    for copy in outs:
        copy.wait()
    for copy in pending:
        copy.wait_send()


def hand_over(*refs):
    count = (len(refs) - 1) // 2
    sems = refs[-1]
    copies = [pltpu.make_async_copy(refs[n], refs[count + n], sems.at[n]) for n in range(count)]
    for copy in copies:
        copy.start()
    for copy in copies:
        copy.wait()


def solution(mesh):
    sizes = tuple(mesh.shape[name] for name in ("tower", "seq", "dp"))
    n_tower, n_seq, n_dp = sizes
    n_z = n_seq // 2
    arows = n_seq * 64
    nr = n_z // 2
    nl = max(n_z - 1 - nr, 1)
    any_spec = pl.BlockSpec(memory_space=pl.ANY)
    vmem = pl.BlockSpec(memory_space=pltpu.VMEM)
    smem = pl.BlockSpec(memory_space=pltpu.SMEM)
    dma = lambda *shape: pltpu.SemaphoreType.DMA(shape)
    low = lambda *shape: pltpu.VMEM(shape, BF16)
    full = lambda *shape: pltpu.VMEM(shape, F32)

    def body(vq, ak, av, aq, vk, vv, up, ao, gains, vlen, alen):
        video = jax.ShapeDtypeStruct((VROWS, WIDTH), BF16)
        audio = jax.ShapeDtypeStruct((64, WIDTH), BF16)
        shapes = (video, audio, video, audio, audio, audio, video, video, jax.ShapeDtypeStruct((4, WIDTH), F32))
        results = pl.pallas_call(
            functools.partial(kernel, sizes),
            out_shape=shapes,
            in_specs=[any_spec] * 8 + [vmem, smem, smem],
            out_specs=tuple([any_spec] * 9),
            scratch_shapes=[
                low(4, arows, WIDTH),
                low(4, VROWS, WIDTH),
                low(2, 64, WIDTH),
                low(VROWS, WIDTH),
                low(VROWS, WIDTH),
                full(2, VROWS, WIDTH),
                low(VROWS, WIDTH),
                low(VROWS, WIDTH),
                low(2, arows, 2 * WIDTH),
                low(2, nr, 128, 2 * WIDTH),
                low(2, nl, 128, 2 * WIDTH),
                low(n_z, 64, 2 * WIDTH),
                low(64, 2 * WIDTH),
                low(64, 2 * WIDTH),
                full(128, 2 * WIDTH),
                low(HEADS, arows, VROWS),
                full(HEADS, arows, VROWS),
                low(arows, VROWS),
                full(HEADS, n_z, 8, VROWS),
                full(n_z, 8, VROWS),
                low(HEADS, VROWS, arows),
                full(HEADS, VROWS, arows),
                low(VROWS, arows),
                full(2, arows, HD),
                full(arows, HD),
                full(VROWS, HD),
                full(2, VROWS, HD),
                full(128, HD),
                full(3, n_tower, 16, HD),
                full(n_z, 16, HD),
                full(n_seq, 16, HD),
                full(8, HD),
                full(n_z, 8, HD),
                full(n_z, 8, HD),
                full(n_seq, 8, HD),
                full(2, 128, HD),
                full(n_seq, 8, WIDTH),
                full(2, 8, WIDTH),
                full(4, WIDTH),
                low(4, 64, WIDTH),
                dma(8), dma(4, n_z), dma(4, n_z), dma(2, n_z), dma(2, n_z), dma(3, n_tower), dma(3, n_tower),
                dma(n_seq), dma(n_seq), dma(n_z), dma(n_z), dma(n_seq), dma(n_seq), dma(n_seq), dma(n_seq),
                dma(1), dma(1), dma(2, HEADS, n_z), dma(2, HEADS, n_z), dma(HEADS, n_z), dma(HEADS, n_z), dma(9),
            ],
            compiler_params=pltpu.CompilerParams(
                collective_id=0, has_side_effects=True, vmem_limit_bytes=58 * 1024 * 1024
            ),
            cost_estimate=pl.CostEstimate(flops=4_800_000_000, bytes_accessed=4_000_000, transcendentals=3_200_000),
        )(vq[0], ak[0], av[0], aq[0], vk[0], vv[0], up[0], ao[0], gains, vlen, alen)
        results = pl.pallas_call(
            hand_over,
            out_shape=shapes,
            in_specs=[any_spec] * 9,
            out_specs=tuple([any_spec] * 9),
            scratch_shapes=[dma(9)],
        )(*results)
        return tuple(r[None] for r in results[:8]) + (results[8],)

    spec = P("dp", "seq", "tower")
    return jax.shard_map(
        body,
        mesh=mesh,
        in_specs=(spec,) * 8 + (P(None, "tower"), P("dp"), P("dp")),
        out_specs=(spec,) * 8 + (P(None, "tower"),),
        check_vma=False,
    )
```

time: 138 us -> 159 us (1.15)
  Pallas kernels: 127 us -> 157 us
  local copies, waits for them, and re-layouts: 7.99 us -> 0 us
    pallas_call x1 -> x2, Pallas kernels: 127 us -> 157 us  [the longest x1 102 us: body(): pl.pallas_call(functools.partial(kernel, sizes), out_shape=shapes, in_spe...]
    unnamed x25 -> x0, local copies, waits for them, and re-layouts: 7.99 us -> none
where the time goes in v2:
time: 159 us
  Pallas kernels  157 us (99%)
  between operations  2.11 us (1%)
    pallas_call x1, Pallas kernels, body(): pl.pallas_call(functools.partial(kernel, sizes), out_shape=shapes, in_spe...  102 us
    pallas_call x1, Pallas kernels, body(): pl.pallas_call(hand_over, out_shape=shapes, in_specs=[any_spec] * 9, out_...  55 us

profile of v2, /device:TPU:8, one launch (start us, length us, event | category | flops | bytes accessed | tf_op | source)
XLA Modules:
  0.0 158.7 jit_solution(15223588763267289422)
XLA Ops:
  1.9 101.6 %shard_map.178 = (bf16[512,384]{1,0:T(8,128)(2,1)}, bf16[64,384]{1,0:T(8,128)(2,1)}, bf16[512,384]{1,0:T(8,128)(2,1)}, bf16[64,384]{1,0:T(8,128)(2,1)}, bf16[64,...) custom-call(bf16[512,384]{1,0:T(8,128)(2,1)} %bitcast.16, ...), custom_call_target="tpu_custom_call" | custom-call | flops 4800000000 | bytes 4000000 | tf_op jit(solution)/shard_map/pallas_call | solution.py:627
  103.5 55.0 %shard_map.179 = (bf16[512,384]{1,0:T(8,128)(2,1)}, bf16[64,384]{1,0:T(8,128)(2,1)}, bf16[512,384]{1,0:T(8,128)(2,1)}, bf16[64,384]{1,0:T(8,128)(2,1)}, bf16[64,...) custom-call(bf16[512,384]{1,0:T(8,128)(2,1)} %get-tuple-element.27.r, ...), custom_call_target="tpu_custom_call" | custom-call | tf_op jit(solution)/shard_map/pallas_call | solution.py:682

commit v3 on v2

--- a/solution.py
+++ b/solution.py
@@ -55,10 +55,10 @@
     sizes,
     vq_h, ak_h, av_h, aq_h, vk_h, vv_h, up_h, ao_h, gains, vlen, alen,
     vo_h, aco_h, vqg_h, akg_h, avg_h, aqg_h, vkg_h, vvg_h, gg_h,
-    g, raw_v, raw_a, qn, kn, dvid, vout, vvg, part, rr, rl, xin, xs, xr, fin,
-    pa, dpa, dsa, ast, acf, pb, dpb, dsb, acc, bias_a, bias_v, rbv, rba, small,
+    g, raw_v, gqn, gkn, qn, kn, dvid, vout, vvg, part, rr, rl, xin, xs, xr, fin,
+    pa, dpa, dsa, ast, acf, pb, dpb, dsb, acc, bias_a, bias_v, rbv, rba, small, fbuf,
     sloc, sin, sres, sall, ub, uin, ucol, gbuf, dbuf, gout, outa,
-    ld, gs, gr, gxs, gxr, ts, tr, s1s, s1r, s2s, s2r, us, ur, ggs, ggr, ds_, dr_,
+    ld, gs, gr, gxs, gxr, ts, tr, fs, fr, s1s, s1r, s2s, s2r, us, ur, ggs, ggr, ds_, dr_,
     rs_s, rs_r, xi_s, xi_r, ost,
 ):
     n_tower, n_seq, n_dp = sizes
@@ -99,8 +99,8 @@
     own = aligned(z * 128 + x * 64, 64, 64)
     loads = []
     for n, (src, dst) in enumerate([
-        (aq_h, raw_a.at[0]),
-        (ak_h, raw_a.at[1]),
+        (aq_h, g.at[2, own]),
+        (ak_h, g.at[3, own]),
         (ao_h, g.at[0, own]),
         (av_h, g.at[1, own]),
         (vq_h, raw_v.at[0]),
@@ -134,7 +134,7 @@
     gbuf[s_at] = jnp.zeros((8, WIDTH), F32)
     loads[0].wait()
     loads[1].wait()
-    both = jnp.concatenate([raw_a[0].astype(F32), raw_a[1].astype(F32)], axis=0)
+    both = jnp.concatenate([g[2, own, :].astype(F32), g[3, own, :].astype(F32)], axis=0)
     small[0, t_at, 8:9, :] = lanes_of(both * both)
     rho = lax.broadcasted_iota(jnp.int32, (arows, HD), 0)
     token = ((rho // 64) % 2) * (n_z * 64) + (rho // 128) * 64 + rho % 64
@@ -204,6 +204,27 @@
     exch = tower_start(0)
     gather_over(1)
     gather_step(0, 0)
+    gather_over(3)
+    gather_step(2, 0)
+
+    everyone = [(delta, k) for delta in range(n_z) for k in range(2) if delta or k]
+    fsent = {}
+
+    def factors_out(row):
+        fbuf[s_at] = jnp.broadcast_to(row, (8, HD))
+        for delta, k in everyone:
+            to = seq_id(1 - x if k else x, z + delta)
+            at = 2 * delta + k
+            fsent[delta, k] = send(fbuf.at[s_at], fbuf.at[s_at], fs.at[at], fr.at[at], seq=to)
+
+    def factors_in(delta):
+        for k in range(2):
+            if delta or k:
+                fsent[-delta % n_z, k].wait_recv()
+
+    def pair_factors(at, n):
+        half = slice(n * 64, n * 64 + 64)
+        return jnp.concatenate([column_of(fbuf[seq_id(xx, at), 0:1, :])[half] for xx in range(2)], axis=0)
 
     stat1 = []
 
@@ -212,10 +233,15 @@
         rows = aligned(at * 128, 128, 128)
         over_wait(0, delta)
         over_wait(2, delta)
+        factors_in(delta)
+        col = pair_factors(at, 0)
+        for h in range(HEADS):
+            cols = head_cols(h)
+            gqn[rows, cols] = (g[2, rows, cols].astype(F32) * col * (gains[2:3, cols] * c)).astype(BF16)
 
         def one(h, carry):
             cols = aligned(h * HD, HD, HD)
-            s = mm(kn[:, cols], g[2, rows, cols], NT) + bias_v[...]
+            s = mm(kn[:, cols], gqn[rows, cols], NT) + bias_v[...]
             m = jnp.maximum(jnp.max(s, axis=0, keepdims=True), FLOOR)
             p = jnp.exp2(s - m)
             dp = mm(raw_v[2, :, cols], g[0, rows, cols], NT)
@@ -239,10 +265,14 @@
     def video_first(delta):
         at = ring(z + delta)
         rows = aligned(at * 128, 128, 128)
+        col = pair_factors(at, 1)
+        for h in range(HEADS):
+            cols = head_cols(h)
+            gkn[rows, cols] = (g[3, rows, cols].astype(F32) * col * gains[1:2, cols]).astype(BF16)
 
         def one(h, carry):
             cols = aligned(h * HD, HD, HD)
-            s = mm(g[3, rows, cols], qn[:, cols], NT) + wide(bias_a[rows, :], 4)
+            s = mm(gkn[rows, cols], qn[:, cols], NT) + wide(bias_a[rows, :], 4)
             m = jnp.maximum(jnp.max(s, axis=0, keepdims=True), FLOOR)
             p = jnp.exp2(s - m)
             dp = mm(g[1, rows, cols], raw_v[3, :, cols], NT)
@@ -254,15 +284,6 @@
             return carry
 
         lax.fori_loop(0, HEADS, one, 0)
-
-    def factor_audio(factors):
-        rba[...] = column_of(factors[8:9, :])
-        for n in range(2):
-            half = slice(n * 64, n * 64 + 64)
-            for h in range(HEADS):
-                cols = head_cols(h)
-                gain = gains[2 - n : 3 - n, cols] * (c if n == 0 else 1.0)
-                g[2 + n, own, cols] = (raw_a[n, :, cols].astype(F32) * rba[half, :] * gain).astype(BF16)
 
     def factor_video(factors):
         for n in range(2):
@@ -275,188 +296,46 @@
                     gain = gains[3 * n : 3 * n + 1, cols] * (c if n == 0 else 1.0)
                     (qn, kn)[n][rows, cols] = (raw_v[n, rows, cols].astype(F32) * col * gain).astype(BF16)
 
-    chains[1, "x", 0].wait_recv()
-    gather_step(1, 0)
-    gather_step(0, 1)
-    factors = lax.rsqrt(tower_sum(0, exch) / depth + EPS)
-    factor_audio(factors)
-    gather_step(2, 0)
-    gather_over(3)
-    factor_video(factors)
-    far = nr
-
-    def maybe(a, k):
-        if k <= far:
-            gather_step(a, k)
-
-    maybe(0, 2)
-    maybe(1, 1)
-    maybe(2, 1)
-    chains[3, "x", 0].wait_recv()
-    gather_step(3, 0)
-    maybe(0, 3)
-    audio_first(0)
-    maybe(1, 2)
-    maybe(2, 2)
-    maybe(3, 1)
-    video_first(0)
-    maybe(0, 4)
-    maybe(1, 3)
-    maybe(2, 3)
-    maybe(3, 2)
+    def maybe(*what):
+        for a, k in what:
+            if k <= nr:
+                gather_step(a, k)
 
     def both_ways(run, dist):
+        if dist > nr:
+            return
+        if dist == 0:
+            run(0)
+            return
         run(-dist)
         if dist <= nl:
             run(dist)
 
+    maybe((0, 1))
+    chains[1, "x", 0].wait_recv()
+    gather_step(1, 0)
+    maybe((2, 1))
+    chains[3, "x", 0].wait_recv()
+    gather_step(3, 0)
+    factors = lax.rsqrt(tower_sum(0, exch) / depth + EPS)
+    factors_out(factors[8:9, :])
+    rba[...] = column_of(factors[8:9, :])
+    factor_video(factors)
+    maybe((0, 2), (2, 2), (1, 1), (3, 1))
+    audio_first(0)
+    maybe((0, 3), (2, 3))
+    video_first(0)
+    maybe((1, 2))
     both_ways(audio_first, 1)
-    maybe(2, 4)
-    maybe(1, 4)
-    maybe(3, 3)
+    maybe((0, 4), (2, 4), (3, 2))
     both_ways(video_first, 1)
-    for dist in range(2, nr + 1):
-        both_ways(audio_first, dist)
-        if dist == 2:
-            maybe(3, 4)
-        both_ways(video_first, dist)
-
-    def video_second(h):
-        cols = head_cols(h)
-        m = ast[h, 0, 0:1, :]
-        for k in range(1, n_z):
-            m = jnp.maximum(m, ast[h, k, 0:1, :])
-        total = jnp.zeros((1, VROWS), F32)
-        inner = jnp.zeros((1, VROWS), F32)
-        for k in range(n_z):
-            f = jnp.exp2(ast[h, k, 0:1, :] - m)
-            acf[k, 0:1, :] = f
-            total = total + f * ast[h, k, 1:2, :]
-            inner = inner + f * ast[h, k, 2:3, :]
-        inverse = 1.0 / total
-        delta = inner * inverse
-
-        def one(k, carry):
-            rows = aligned(k * 128, 128, 128)
-            w = pa[h, rows, :].astype(F32) * (acf[k, 0:1, :] * inverse)
-            pa[h, rows, :] = w.astype(BF16)
-            dsa[rows, :] = (w * (dpa[h, rows, :] - delta)).astype(BF16)
-            return carry
-
-        lax.fori_loop(0, n_z, one, 0)
-        low = pa[h]
-        ds = dsa[...]
-        dk = mm(ds, qn[:, cols], NN) * unscale
-        part[0, :, h * 256 : h * 256 + HD] = dk.astype(BF16)
-        part[0, :, h * 256 + HD : h * 256 + 256] = mm(low, raw_v[3, :, cols], NN).astype(BF16)
-        prod = dk * g[3, :, cols].astype(F32)
-        gbuf[s_at, 1:2, cols] = jnp.sum(prod, axis=0, keepdims=True) / gains[1:2, cols]
-        acc[0] = prod if h == 0 else acc[0] + prod
-        vout[:, cols] = mm(g[1, :, cols], low, TN).T.astype(BF16)
-        dvid[0, :, cols] = mm(g[3, :, cols], ds, TN).T * scale
-
-    tile = 256
-    tiles = arows // tile
-
-    def audio_second(h):
-        cols = head_cols(h)
-
-        def one(t, carry):
-            lanes = aligned(t * tile, tile, tile)
-
-            def stat(ref, at):
-                return jnp.concatenate([ref[t * 2, at : at + 1, :], ref[t * 2 + 1, at : at + 1, :]], axis=1)
-
-            coef = jnp.exp2(stat(sloc, h) - stat(sall, h))
-            delta = stat(sall, 3 + h)
-            w = pb[h, :, lanes].astype(F32) * coef
-            pb[h, :, lanes] = w.astype(BF16)
-            dsb[:, lanes] = (w * (dpb[h, :, lanes] - delta)).astype(BF16)
-            return carry
-
-        lax.fori_loop(0, tiles, one, 0)
-        low = pb[h]
-        ds = dsb[...]
-        part[1, :, h * 256 : h * 256 + HD] = mm(raw_v[2, :, cols], low, TN).T.astype(BF16)
-        dq = mm(kn[:, cols], ds, TN).T * scale
-        part[1, :, h * 256 + HD : h * 256 + 256] = dq.astype(BF16)
-        prod = dq * g[2, :, cols].astype(F32) * (1.0 / c)
-        gbuf[s_at, 2:3, cols] = jnp.sum(prod, axis=0, keepdims=True) / gains[2:3, cols]
-        acc[1] = prod if h == 0 else acc[1] + prod
-        dvid[1, :, cols] = mm(ds, g[2, :, cols], NN) * unscale
-        vvg[:, cols] = mm(low, g[0, :, cols], NN).astype(BF16)
-
-    rchain = {}
-
-    def group(h):
-        return slice(h * 256, (h + 1) * 256)
-
-    def scatter_over(h):
-        for k, delta in enumerate(order):
-            at = ring(z + delta)
-            rchain[h, "x", delta % n_z] = send(
-                part.at[1, aligned(at * 128 + (1 - x) * 64, 64, 64), group(h)],
-                xin.at[at, :, group(h)],
-                xi_s.at[h, k], xi_r.at[h, k], seq=over,
-            )
-
-    order = []
-    for dist in range(nr, 0, -1):
-        order.append(dist)
-        if dist <= nl:
-            order.append(-dist)
-    order.append(0)
-
-    def scatter_step(b, h, k):
-        cols = group(h)
-        for name, n, to, way, base, land in (("r", nr, right, 1, 0, rr), ("l", nl, left, -1, nr, rl)):
-            if k >= n:
-                continue
-            delta = way * (n - k)
-            at = ring(z + delta)
-            size = 128 if b == 0 else 64
-            rows = aligned(at * 128, 128, 128) if b == 0 else aligned(at * 128 + x * 64, 64, 64)
-            if b == 1 or k > 0:
-                total = part[b, rows, cols].astype(F32)
-                if b == 1:
-                    rchain[h, "x", delta % n_z].wait_recv()
-                    total = total + xin[at, :, cols].astype(F32)
-                if k > 0:
-                    rchain[b, h, name, k - 1].wait_recv()
-                    total = total + land[b, k - 1, 0:size, cols].astype(F32)
-                part[b, rows, cols] = total.astype(BF16)
-            rchain[b, h, name, k] = send(
-                part.at[b, rows, cols], land.at[b, k, 0:size, cols],
-                rs_s.at[b, h, base + k], rs_r.at[b, h, base + k], seq=to,
-            )
-
-    def scatter_landed(b, h, total, size):
-        cols = group(h)
-        rchain[b, h, "r", nr - 1].wait_recv()
-        total = total + rr[b, nr - 1, 0:size, cols].astype(F32)
-        if nl > 0:
-            rchain[b, h, "l", nl - 1].wait_recv()
-            total = total + rl[b, nl - 1, 0:size, cols].astype(F32)
-        return total
-
-    def key_cross(h):
-        cols = group(h)
-        fin[:, cols] = scatter_landed(0, h, part[0, aligned(z * 128, 128, 128), cols].astype(F32), 128)
-        xs[:, cols] = fin[aligned((1 - x) * 64, 64, 64), cols].astype(BF16)
-        rchain[h, "k"] = send(xs.at[:, cols], xr.at[:, cols], rs_s.at[0, h, n_z - 1], rs_r.at[0, h, n_z - 1], seq=over)
-
-    def key_end(h):
-        cols = group(h)
-        rchain[h, "k"].wait_recv()
-        return fin[aligned(x * 64, 64, 64), cols] + xr[:, cols].astype(F32)
-
-    def query_end(h):
-        cols = group(h)
-        rchain[h, "x", 0].wait_recv()
-        return scatter_landed(1, h, part[1, own, cols].astype(F32) + xin[z, :, cols].astype(F32), 64)
-
-    video_second(0)
-    scatter_step(0, 0, 0)
+    both_ways(audio_first, 2)
+    maybe((1, 3), (3, 3))
+    both_ways(video_first, 2)
+    both_ways(audio_first, 3)
+    both_ways(audio_first, 4)
+    maybe((1, 4), (3, 4))
+    both_ways(video_first, 3)
 
     for copy in stat1:
         copy.wait_recv()
@@ -473,28 +352,160 @@
     sres[3:6, :] = inn / tot
     stat2 = [send(sres, sall.at[z], s2s.at[k], s2r.at[k], seq=seq_id(x, z + k)) for k in range(1, n_z)]
     sall[z] = sres[...]
-
-    def steps(b, at):
-        for h in range(HEADS):
-            k = at - h
-            if 0 <= k < nr:
-                scatter_step(b, h, k)
-
+    both_ways(video_first, 4)
+
+    def video_second(h):
+        cols = head_cols(h)
+        m = ast[h, 0, 0:1, :]
+        for k in range(1, n_z):
+            m = jnp.maximum(m, ast[h, k, 0:1, :])
+        total = jnp.zeros((1, VROWS), F32)
+        inner = jnp.zeros((1, VROWS), F32)
+        for k in range(n_z):
+            f = jnp.exp2(ast[h, k, 0:1, :] - m)
+            acf[k, 0:1, :] = f
+            total = total + f * ast[h, k, 1:2, :]
+            inner = inner + f * ast[h, k, 2:3, :]
+        inverse = 1.0 / total
+        delta = inner * inverse
+
+        def one(k, carry):
+            rows = aligned(k * 128, 128, 128)
+            w = pa[h, rows, :].astype(F32) * (acf[k, 0:1, :] * inverse)
+            pa[h, rows, :] = w.astype(BF16)
+            dsa[rows, :] = (w * (dpa[h, rows, :] - delta)).astype(BF16)
+            return carry
+
+        lax.fori_loop(0, n_z, one, 0)
+        low = pa[h]
+        ds = dsa[...]
+        dk = mm(ds, qn[:, cols], NN) * unscale
+        part[h, :, 0:HD] = dk.astype(BF16)
+        part[h, :, HD:] = mm(low, raw_v[3, :, cols], NN).astype(BF16)
+        prod = dk * gkn[:, cols].astype(F32)
+        gbuf[s_at, 1:2, cols] = jnp.sum(prod, axis=0, keepdims=True) / gains[1:2, cols]
+        acc[0] = prod if h == 0 else acc[0] + prod
+        vout[:, cols] = mm(g[1, :, cols], low, TN).T.astype(BF16)
+        dvid[0, :, cols] = mm(gkn[:, cols], ds, TN).T * scale
+
+    tile = 256
+    tiles = arows // tile
+
+    def audio_second(h):
+        cols = head_cols(h)
+
+        def one(t, carry):
+            lanes = aligned(t * tile, tile, tile)
+
+            def stat(ref, at):
+                return jnp.concatenate([ref[t * 2, at : at + 1, :], ref[t * 2 + 1, at : at + 1, :]], axis=1)
+
+            coef = jnp.exp2(stat(sloc, h) - stat(sall, h))
+            delta = stat(sall, 3 + h)
+            w = pb[h, :, lanes].astype(F32) * coef
+            pb[h, :, lanes] = w.astype(BF16)
+            dsb[:, lanes] = (w * (dpb[h, :, lanes] - delta)).astype(BF16)
+            return carry
+
+        lax.fori_loop(0, tiles, one, 0)
+        low = pb[h]
+        ds = dsb[...]
+        part[HEADS + h, :, 0:HD] = mm(raw_v[2, :, cols], low, TN).T.astype(BF16)
+        dq = mm(kn[:, cols], ds, TN).T * scale
+        part[HEADS + h, :, HD:] = dq.astype(BF16)
+        prod = dq * gqn[:, cols].astype(F32) * (1.0 / c)
+        gbuf[s_at, 2:3, cols] = jnp.sum(prod, axis=0, keepdims=True) / gains[2:3, cols]
+        acc[1] = prod if h == 0 else acc[1] + prod
+        dvid[1, :, cols] = mm(ds, gqn[:, cols], NN) * unscale
+        vvg[:, cols] = mm(low, g[0, :, cols], NN).astype(BF16)
+
+    over_first = (0, HEADS + 1, HEADS + 2)
+    mirrored = (0, 2, HEADS + 2)
+    rchain = {}
+    order = []
+    for dist in range(nr, 0, -1):
+        order.append(dist)
+        if dist <= nl:
+            order.append(-dist)
+    order.append(0)
+
+    def scatter_over(*units):
+        for k in range(n_z):
+            for u in units:
+                delta = -order[k] if u in mirrored else order[k]
+                at = ring(z + delta)
+                rchain[u, "x", delta % n_z] = send(
+                    part.at[u, aligned(at * 128 + (1 - x) * 64, 64, 64)], xin.at[u, at],
+                    xi_s.at[u, k], xi_r.at[u, k], seq=over,
+                )
+
+    def scatter_step(*what):
+        for u, k in what:
+            early = u in over_first
+            way = -1 if u in mirrored else 1
+            size = 64 if early else 128
+            ends = (right, left)[::way]
+            for name, n, to, sign, base, land in (
+                ("l", nr, ends[0], way, 0, rr), ("s", nl, ends[1], -way, nr, rl),
+            ):
+                if k >= n:
+                    continue
+                delta = sign * (n - k)
+                at = ring(z + delta)
+                rows = aligned(at * 128 + x * 64, 64, 64) if early else aligned(at * 128, 128, 128)
+                if early or k > 0:
+                    total = part[u, rows, :].astype(F32)
+                    if early:
+                        rchain[u, "x", delta % n_z].wait_recv()
+                        total = total + xin[u, at].astype(F32)
+                    if k > 0:
+                        rchain[u, name, k - 1].wait_recv()
+                        total = total + land[u, k - 1, 0:size, :].astype(F32)
+                    part[u, rows, :] = total.astype(BF16)
+                rchain[u, name, k] = send(
+                    part.at[u, rows], land.at[u, k, 0:size], rs_s.at[u, base + k], rs_r.at[u, base + k], seq=to
+                )
+
+    def landed(u, total, size):
+        rchain[u, "l", nr - 1].wait_recv()
+        total = total + rr[u, nr - 1, 0:size, :].astype(F32)
+        if nl > 0:
+            rchain[u, "s", nl - 1].wait_recv()
+            total = total + rl[u, nl - 1, 0:size, :].astype(F32)
+        return total
+
+    def scatter_cross(*units):
+        for u in units:
+            fin[u] = landed(u, part[u, aligned(z * 128, 128, 128), :].astype(F32), 128)
+            xs[u] = fin[u, aligned((1 - x) * 64, 64, 64), :].astype(BF16)
+            rchain[u, "k"] = send(xs.at[u], xr.at[u], rs_s.at[u, n_z - 1], rs_r.at[u, n_z - 1], seq=over)
+
+    def scatter_end(u):
+        if u in over_first:
+            rchain[u, "x", 0].wait_recv()
+            return landed(u, part[u, own, :].astype(F32) + xin[u, z].astype(F32), 64)
+        rchain[u, "k"].wait_recv()
+        return fin[u, aligned(x * 64, 64, 64), :] + xr[u].astype(F32)
+
+    def steps(*what):
+        scatter_step(*[(u, k) for u, k in what if k < nr])
+
+    video_second(0)
+    scatter_over(0)
     video_second(1)
-    steps(0, 1)
+    steps((1, 0))
     video_second(2)
-    steps(0, 2)
+    steps((2, 0))
+    steps((0, 0))
     for copy in stat2:
         copy.wait_recv()
     audio_second(0)
-    scatter_over(0)
-    steps(0, 3)
+    steps((3, 0), (1, 1), (2, 1), (0, 1))
     audio_second(1)
-    scatter_over(1)
-    steps(0, 4)
+    scatter_over(4)
     audio_second(2)
-    scatter_over(2)
-    steps(0, 5)
+    scatter_over(5)
+    steps((3, 1), (1, 2), (2, 2), (0, 2))
 
     for n, row in ((0, 0), (1, 3)):
         inner = dvid[n] * (qn, kn)[n][...].astype(F32) * (1.0 / c if n == 0 else 1.0)
@@ -523,10 +534,7 @@
 
     write(vout, vo_h)
     write(vvg, vvg_h)
-    steps(1, 0)
-    for h in range(HEADS):
-        key_cross(h)
-    steps(1, 1)
+    steps((4, 0), (5, 0), (1, 3), (2, 3), (3, 2), (0, 3), (4, 1), (5, 1))
 
     inner = tower_sum(1, exch) * (1.0 / depth)
 
@@ -543,7 +551,7 @@
         write((qn, kn)[n], (vqg_h, vkg_h)[n])
 
     video_grad(0)
-    steps(1, 2)
+    steps((3, 3), (4, 2), (5, 2))
     for copy in ucopies:
         copy.wait_recv()
     total = uin[0]
@@ -552,7 +560,9 @@
     small[2, t_at, 0:8, :] = total
     uexch = tower_start(2)
     video_grad(1)
-    steps(1, 3)
+    scatter_cross(1, 2)
+    steps((4, 3), (5, 3))
+    scatter_cross(3)
     for copy in gcopies:
         copy.wait_recv()
     total = gbuf[0]
@@ -561,7 +571,6 @@
     if n_dp > 1:
         dbuf[d_at] = total
         gcopy = send(dbuf.at[d_at], dbuf.at[d_at], ds_.at[0], dr_.at[0], dp=1 - d_at)
-    steps(1, 4)
     uall = tower_sum(2, uexch) * (1.0 / depth)
     for n in range(2):
         ucol[n] = column_of(uall[n : n + 1, :])
@@ -570,22 +579,21 @@
         cols = head_cols(h)
         r = rba[(1 - n) * 64 : (2 - n) * 64, :]
         col = ucol[n, aligned(x * 64, 64, 64), :]
-        return (r * gains[n + 1 : n + 2, cols] * total - raw_a[1 - n, :, cols].astype(F32) * (r * r * col)).astype(BF16)
-
-    for h in range(HEADS):
-        both = key_end(h)
-        outa[2, :, head_cols(h)] = audio_grad(0, h, both[:, 0:HD])
-        outa[3, :, head_cols(h)] = both[:, HD:].astype(BF16)
-    write(outa.at[2], akg_h)
-    write(outa.at[3], avg_h)
+        return (r * gains[n + 1 : n + 2, cols] * total - g[3 - n, own, cols].astype(F32) * (r * r * col)).astype(BF16)
+
     if n_dp > 1:
         gcopy.wait_recv()
         total = dbuf[0] + dbuf[1]
     gout[...] = total[0:4, :]
     write(gout, gg_h)
-    steps(1, 5)
     for h in range(HEADS):
-        both = query_end(h)
+        both = scatter_end(h)
+        outa[2, :, head_cols(h)] = audio_grad(0, h, both[:, 0:HD])
+        outa[3, :, head_cols(h)] = both[:, HD:].astype(BF16)
+    write(outa.at[2], akg_h)
+    write(outa.at[3], avg_h)
+    for h in range(HEADS):
+        both = scatter_end(HEADS + h)
         outa[0, :, head_cols(h)] = both[:, 0:HD].astype(BF16)
         outa[1, :, head_cols(h)] = audio_grad(1, h, both[:, HD:])
     write(outa.at[0], aco_h)
@@ -632,19 +640,20 @@
             scratch_shapes=[
                 low(4, arows, WIDTH),
                 low(4, VROWS, WIDTH),
-                low(2, 64, WIDTH),
+                low(arows, WIDTH),
+                low(arows, WIDTH),
                 low(VROWS, WIDTH),
                 low(VROWS, WIDTH),
                 full(2, VROWS, WIDTH),
                 low(VROWS, WIDTH),
                 low(VROWS, WIDTH),
-                low(2, arows, 2 * WIDTH),
-                low(2, nr, 128, 2 * WIDTH),
-                low(2, nl, 128, 2 * WIDTH),
-                low(n_z, 64, 2 * WIDTH),
-                low(64, 2 * WIDTH),
-                low(64, 2 * WIDTH),
-                full(128, 2 * WIDTH),
+                low(6, arows, 256),
+                low(6, nr, 128, 256),
+                low(6, nl, 128, 256),
+                low(6, n_z, 64, 256),
+                low(6, 64, 256),
+                low(6, 64, 256),
+                full(6, 128, 256),
                 low(HEADS, arows, VROWS),
                 full(HEADS, arows, VROWS),
                 low(arows, VROWS),
@@ -659,6 +668,7 @@
                 full(2, VROWS, HD),
                 full(128, HD),
                 full(3, n_tower, 16, HD),
+                full(n_seq, 8, HD),
                 full(n_z, 16, HD),
                 full(n_seq, 16, HD),
                 full(8, HD),
@@ -671,8 +681,8 @@
                 full(4, WIDTH),
                 low(4, 64, WIDTH),
                 dma(8), dma(4, n_z), dma(4, n_z), dma(2, n_z), dma(2, n_z), dma(3, n_tower), dma(3, n_tower),
-                dma(n_seq), dma(n_seq), dma(n_z), dma(n_z), dma(n_seq), dma(n_seq), dma(n_seq), dma(n_seq),
-                dma(1), dma(1), dma(2, HEADS, n_z), dma(2, HEADS, n_z), dma(HEADS, n_z), dma(HEADS, n_z), dma(9),
+                dma(n_seq), dma(n_seq), dma(n_seq), dma(n_seq), dma(n_z), dma(n_z), dma(n_seq), dma(n_seq),
+                dma(n_seq), dma(n_seq), dma(1), dma(1), dma(6, n_z), dma(6, n_z), dma(6, n_z), dma(6, n_z), dma(9),
             ],
             compiler_params=pltpu.CompilerParams(
                 collective_id=0, has_side_effects=True, vmem_limit_bytes=58 * 1024 * 1024
@@ -682,7 +692,7 @@
         results = pl.pallas_call(
             hand_over,
             out_shape=shapes,
-            in_specs=[any_spec] * 9,
+            in_specs=[vmem] * 9,
             out_specs=tuple([any_spec] * 9),
             scratch_shapes=[dma(9)],
         )(*results)

time: 159 us -> 94.3 us (0.59)
  Pallas kernels: 157 us -> 91.4 us
    pallas_call x1, Pallas kernels: 55 us -> 2.75 us  [body(): pl.pallas_call(hand_over, out_shape=shapes, in_specs=[vmem] * 9, out_spec...]
    pallas_call x1, Pallas kernels: 102 us -> 88.6 us  [body(): pl.pallas_call(functools.partial(kernel, sizes), out_shape=shapes, in_spe...]
where the time goes in v3:
time: 94.3 us; the launch traced here: 93.5 us
  Pallas kernels  91.4 us (97%)
  between operations  2.11 us (2%)
    pallas_call x1, Pallas kernels, body(): pl.pallas_call(functools.partial(kernel, sizes), out_shape=shapes, in_spe...  88.6 us
    pallas_call x1, Pallas kernels, body(): pl.pallas_call(hand_over, out_shape=shapes, in_specs=[vmem] * 9, out_spec...  2.75 us

profile of v3, /device:TPU:8, one launch (start us, length us, event | category | flops | bytes accessed | tf_op | source)
XLA Modules:
  0.0 93.5 jit_solution(4832098221071289970)
XLA Ops:
  1.9 88.6 %shard_map.178 = (bf16[512,384]{1,0:T(8,128)(2,1)}, bf16[64,384]{1,0:T(8,128)(2,1)}, bf16[512,384]{1,0:T(8,128)(2,1)}, bf16[64,384]{1,0:T(8,128)(2,1)}, bf16[64,...) custom-call(bf16[512,384]{1,0:T(8,128)(2,1)} %bitcast.16, ...), custom_call_target="tpu_custom_call" | custom-call | flops 4800000000 | bytes 4000000 | tf_op jit(solution)/shard_map/pallas_call | solution.py:635
  90.6 2.7 %shard_map.179 = (bf16[512,384]{1,0:T(8,128)(2,1)}, bf16[64,384]{1,0:T(8,128)(2,1)}, bf16[512,384]{1,0:T(8,128)(2,1)}, bf16[64,384]{1,0:T(8,128)(2,1)}, bf16[64,...) custom-call(bf16[512,384]{1,0:T(8,128)(2,1)} %get-tuple-element.27.r, ...), custom_call_target="tpu_custom_call" | custom-call | tf_op jit(solution)/shard_map/pallas_call | solution.py:692

commit v4 on v3

--- a/solution.py
+++ b/solution.py
@@ -126,26 +126,7 @@
         for k in range(4):
             small[n, t_at, which * 4 + k : which * 4 + k + 1, :] = row[:, k * HD : (k + 1) * HD]
 
-    for n in range(3):
-        small[n, t_at] = jnp.zeros((16, HD), F32)
-    sloc[...] = jnp.zeros_like(sloc)
-    sres[...] = jnp.zeros_like(sres)
-    ub[...] = jnp.zeros_like(ub)
-    gbuf[s_at] = jnp.zeros((8, WIDTH), F32)
-    loads[0].wait()
-    loads[1].wait()
-    both = jnp.concatenate([g[2, own, :].astype(F32), g[3, own, :].astype(F32)], axis=0)
-    small[0, t_at, 8:9, :] = lanes_of(both * both)
-    rho = lax.broadcasted_iota(jnp.int32, (arows, HD), 0)
-    token = ((rho // 64) % 2) * (n_z * 64) + (rho // 128) * 64 + rho % 64
-    bias_a[...] = jnp.where(token < alen[0], 0.0, MASKED)
-    vtok = s_at * VROWS + lax.broadcasted_iota(jnp.int32, (VROWS, HD), 0)
-    bias_v[...] = jnp.where(vtok < vlen[0], 0.0, MASKED)
-    for n in range(2):
-        loads[4 + n].wait()
-        widened = raw_v[n].astype(F32)
-        put_video(0, n, lanes_of(widened * widened))
-    for n in (2, 3, 6, 7):
+    for n in range(4):
         loads[n].wait()
     pl.semaphore_wait(barrier, peers)
 
@@ -163,49 +144,81 @@
             total = total + small[n, k]
         return total
 
+    arrays = (0, 2, 1, 3, 1, 3)
     chains = {}
 
-    def gather_step(a, k):
-        last_over = a % 2 == 0
-        sign = 1 if a >= 2 else -1
-        ways = (("l", nr, left if a >= 2 else right, sign, 0), ("s", nl, right if a >= 2 else left, -sign, nr))
+    def gather_step(n, k):
+        a = arrays[n]
+        sign = 1 if n % 2 else -1
+        ways = (("l", nr, left if n % 2 else right, sign, 0), ("s", nl, right if n % 2 else left, -sign, nr))
+        half = 1 - x if n >= 4 else x
 
         def block(zz):
-            if last_over:
-                return g.at[a, aligned(ring(zz) * 128 + x * 64, 64, 64)]
-            return g.at[a, aligned(ring(zz) * 128, 128, 128)]
-
-        if k == 0 and last_over:
-            chains[a, "x", 0] = send(block(z), block(z), gxs.at[a // 2, 0], gxr.at[a // 2, 0], seq=over)
-        for name, n, to, way, base in ways:
-            if k > n:
+            return g.at[a, aligned(ring(zz) * 128 + half * 64, 64, 64)]
+
+        if k == 0 and n >= 4:
+            chains[n - 2, "x", 0].wait_recv()
+        for name, count, to, way, base in ways:
+            if k > count:
                 continue
             here = block(z + way * k)
             if k > 0:
-                chains[a, name, k].wait_recv()
-            if k < n:
-                chains[a, name, k + 1] = send(here, here, gs.at[a, 1 + base + k], gr.at[a, 1 + base + k], seq=to)
-            if k > 0 and last_over:
-                chains[a, "x", base + k] = send(here, here, gxs.at[a // 2, base + k], gxr.at[a // 2, base + k], seq=over)
-
-    def gather_over(a):
-        chains[a, "x", 0] = send(g.at[a, own], g.at[a, own], gs.at[a, 0], gr.at[a, 0], seq=over)
-
-    def over_wait(a, delta):
-        towards = delta if a >= 2 else -delta
+                chains[n, name, k].wait_recv()
+            if k < count:
+                chains[n, name, k + 1] = send(here, here, gs.at[n, base + k], gr.at[n, base + k], seq=to)
+            if k > 0 and n < 2:
+                chains[n, "x", base + k] = send(here, here, gxs.at[n, base + k], gxr.at[n, base + k], seq=over)
+
+    def gather_over(n):
+        here = g.at[arrays[n], own]
+        chains[n, "x", 0] = send(here, here, gxs.at[n, 0], gxr.at[n, 0], seq=over)
+
+    def over_wait(n, delta):
+        towards = delta if n % 2 else -delta
         if delta == 0:
             at = 0
         elif abs(delta) == nr or towards > 0:
             at = abs(delta)
         else:
             at = nr + abs(delta)
-        chains[a, "x", at].wait_recv()
-
+        chains[n, "x", at].wait_recv()
+
+    def gather(*what):
+        for n, k in what:
+            if k <= nr:
+                gather_step(n, k)
+
+    gather_over(2)
+    gather_over(3)
+    gather((0, 0), (1, 0), (2, 0), (3, 0))
+    gather_over(0)
+    gather_over(1)
+
+    def put_video(n, which, row):
+        for k in range(4):
+            small[n, t_at, which * 4 + k : which * 4 + k + 1, :] = row[:, k * HD : (k + 1) * HD]
+
+    for n in range(3):
+        small[n, t_at] = jnp.zeros((16, HD), F32)
+    both = jnp.concatenate([g[2, own, :].astype(F32), g[3, own, :].astype(F32)], axis=0)
+    small[0, t_at, 8:9, :] = lanes_of(both * both)
+    for n in range(2):
+        loads[4 + n].wait()
+        widened = raw_v[n].astype(F32)
+        put_video(0, n, lanes_of(widened * widened))
     exch = tower_start(0)
-    gather_over(1)
-    gather_step(0, 0)
-    gather_over(3)
-    gather_step(2, 0)
+    gather((4, 0), (5, 0), (0, 1), (1, 1))
+    sloc[...] = jnp.zeros_like(sloc)
+    sres[...] = jnp.zeros_like(sres)
+    ub[...] = jnp.zeros_like(ub)
+    gbuf[s_at] = jnp.zeros((8, WIDTH), F32)
+    rho = lax.broadcasted_iota(jnp.int32, (arows, HD), 0)
+    token = ((rho // 64) % 2) * (n_z * 64) + (rho // 128) * 64 + rho % 64
+    bias_a[...] = jnp.where(token < alen[0], 0.0, MASKED)
+    vtok = s_at * VROWS + lax.broadcasted_iota(jnp.int32, (VROWS, HD), 0)
+    bias_v[...] = jnp.where(vtok < vlen[0], 0.0, MASKED)
+    for n in (6, 7):
+        loads[n].wait()
 
     everyone = [(delta, k) for delta in range(n_z) for k in range(2) if delta or k]
     fsent = {}
@@ -228,62 +241,57 @@
 
     stat1 = []
 
-    def audio_first(delta):
-        at = ring(z + delta)
-        rows = aligned(at * 128, 128, 128)
-        over_wait(0, delta)
-        over_wait(2, delta)
-        factors_in(delta)
-        col = pair_factors(at, 0)
-        for h in range(HEADS):
-            cols = head_cols(h)
-            gqn[rows, cols] = (g[2, rows, cols].astype(F32) * col * (gains[2:3, cols] * c)).astype(BF16)
-
-        def one(h, carry):
-            cols = aligned(h * HD, HD, HD)
-            s = mm(kn[:, cols], gqn[rows, cols], NT) + bias_v[...]
-            m = jnp.maximum(jnp.max(s, axis=0, keepdims=True), FLOOR)
-            p = jnp.exp2(s - m)
-            dp = mm(raw_v[2, :, cols], g[0, rows, cols], NT)
-            pb[h, :, rows] = p.astype(BF16)
-            dpb[h, :, rows] = dp
-            sloc[at, pl.ds(h, 1), :] = m
-            sloc[at, pl.ds(3 + h, 1), :] = jnp.sum(p, axis=0, keepdims=True)
-            sloc[at, pl.ds(6 + h, 1), :] = jnp.sum(p * dp, axis=0, keepdims=True)
-            return carry
-
-        lax.fori_loop(0, HEADS, one, 0)
-        slot = delta % n_z
-        for k, xx in enumerate((x, 1 - x)):
-            if delta == 0 and k == 0:
-                sin[s_at] = sloc[at]
-            else:
-                stat1.append(
-                    send(sloc.at[at], sin.at[s_at], s1s.at[2 * slot + k], s1r.at[2 * slot + k], seq=seq_id(xx, at))
-                )
-
-    def video_first(delta):
-        at = ring(z + delta)
-        rows = aligned(at * 128, 128, 128)
-        col = pair_factors(at, 1)
-        for h in range(HEADS):
-            cols = head_cols(h)
-            gkn[rows, cols] = (g[3, rows, cols].astype(F32) * col * gains[1:2, cols]).astype(BF16)
-
-        def one(h, carry):
-            cols = aligned(h * HD, HD, HD)
-            s = mm(gkn[rows, cols], qn[:, cols], NT) + wide(bias_a[rows, :], 4)
-            m = jnp.maximum(jnp.max(s, axis=0, keepdims=True), FLOOR)
-            p = jnp.exp2(s - m)
-            dp = mm(g[1, rows, cols], raw_v[3, :, cols], NT)
-            pa[h, rows, :] = p.astype(BF16)
-            dpa[h, rows, :] = dp
-            ast[h, at, 0:1, :] = m
-            ast[h, at, 1:2, :] = jnp.sum(p, axis=0, keepdims=True)
-            ast[h, at, 2:3, :] = jnp.sum(p * dp, axis=0, keepdims=True)
-            return carry
-
-        lax.fori_loop(0, HEADS, one, 0)
+    def audio_first(*deltas):
+        for delta in deltas:
+            over_wait(0, delta)
+            over_wait(1, delta)
+            factors_in(delta)
+        for delta in deltas:
+            at = ring(z + delta)
+            rows = aligned(at * 128, 128, 128)
+            col = pair_factors(at, 0)
+            for h in range(HEADS):
+                cols = head_cols(h)
+                query = (g[2, rows, cols].astype(F32) * col * (gains[2:3, cols] * c)).astype(BF16)
+                gqn[rows, cols] = query
+                s = mm(kn[:, cols], query, NT) + bias_v[...]
+                m = jnp.maximum(jnp.max(s, axis=0, keepdims=True), FLOOR)
+                p = jnp.exp2(s - m)
+                dp = mm(raw_v[2, :, cols], g[0, rows, cols], NT)
+                pb[h, :, rows] = p.astype(BF16)
+                dpb[h, :, rows] = dp
+                sloc[at, h : h + 1, :] = m
+                sloc[at, 3 + h : 4 + h, :] = jnp.sum(p, axis=0, keepdims=True)
+                sloc[at, 6 + h : 7 + h, :] = jnp.sum(p * dp, axis=0, keepdims=True)
+        for delta in deltas:
+            at = ring(z + delta)
+            slot = delta % n_z
+            for k, xx in enumerate((x, 1 - x)):
+                if delta == 0 and k == 0:
+                    sin[s_at] = sloc[at]
+                else:
+                    n = 2 * slot + k
+                    stat1.append(send(sloc.at[at], sin.at[s_at], s1s.at[n], s1r.at[n], seq=seq_id(xx, at)))
+
+    def video_first(*deltas):
+        for delta in deltas:
+            at = ring(z + delta)
+            rows = aligned(at * 128, 128, 128)
+            col = pair_factors(at, 1)
+            bias = wide(bias_a[rows, :], 4)
+            for h in range(HEADS):
+                cols = head_cols(h)
+                key = (g[3, rows, cols].astype(F32) * col * gains[1:2, cols]).astype(BF16)
+                gkn[rows, cols] = key
+                s = mm(key, qn[:, cols], NT) + bias
+                m = jnp.maximum(jnp.max(s, axis=0, keepdims=True), FLOOR)
+                p = jnp.exp2(s - m)
+                dp = mm(g[1, rows, cols], raw_v[3, :, cols], NT)
+                pa[h, rows, :] = p.astype(BF16)
+                dpa[h, rows, :] = dp
+                ast[h, at, 0:1, :] = m
+                ast[h, at, 1:2, :] = jnp.sum(p, axis=0, keepdims=True)
+                ast[h, at, 2:3, :] = jnp.sum(p * dp, axis=0, keepdims=True)
 
     def factor_video(factors):
         for n in range(2):
@@ -296,45 +304,29 @@
                     gain = gains[3 * n : 3 * n + 1, cols] * (c if n == 0 else 1.0)
                     (qn, kn)[n][rows, cols] = (raw_v[n, rows, cols].astype(F32) * col * gain).astype(BF16)
 
-    def maybe(*what):
-        for a, k in what:
-            if k <= nr:
-                gather_step(a, k)
-
     def both_ways(run, dist):
-        if dist > nr:
-            return
-        if dist == 0:
-            run(0)
-            return
-        run(-dist)
-        if dist <= nl:
-            run(dist)
-
-    maybe((0, 1))
-    chains[1, "x", 0].wait_recv()
-    gather_step(1, 0)
-    maybe((2, 1))
-    chains[3, "x", 0].wait_recv()
-    gather_step(3, 0)
+        if dist < nr or dist <= nl:
+            run(-dist, dist)
+        elif dist == nr:
+            run(-dist)
+
     factors = lax.rsqrt(tower_sum(0, exch) / depth + EPS)
     factors_out(factors[8:9, :])
+    gather((2, 1), (3, 1))
     rba[...] = column_of(factors[8:9, :])
     factor_video(factors)
-    maybe((0, 2), (2, 2), (1, 1), (3, 1))
+    gather((4, 1), (5, 1), (0, 2), (1, 2))
     audio_first(0)
-    maybe((0, 3), (2, 3))
+    gather((2, 2), (3, 2), (4, 2), (5, 2), (0, 3), (1, 3))
+    both_ways(audio_first, 1)
     video_first(0)
-    maybe((1, 2))
-    both_ways(audio_first, 1)
-    maybe((0, 4), (2, 4), (3, 2))
+    gather((2, 3), (3, 3), (0, 4), (1, 4), (4, 3), (5, 3))
     both_ways(video_first, 1)
     both_ways(audio_first, 2)
-    maybe((1, 3), (3, 3))
     both_ways(video_first, 2)
     both_ways(audio_first, 3)
     both_ways(audio_first, 4)
-    maybe((1, 4), (3, 4))
+    gather((2, 4), (3, 4))
     both_ways(video_first, 3)
 
     for copy in stat1:
@@ -352,6 +344,7 @@
     sres[3:6, :] = inn / tot
     stat2 = [send(sres, sall.at[z], s2s.at[k], s2r.at[k], seq=seq_id(x, z + k)) for k in range(1, n_z)]
     sall[z] = sres[...]
+    gather((4, 4), (5, 4))
     both_ways(video_first, 4)
 
     def video_second(h):
@@ -369,14 +362,11 @@
         inverse = 1.0 / total
         delta = inner * inverse
 
-        def one(k, carry):
-            rows = aligned(k * 128, 128, 128)
+        for k in range(n_z):
+            rows = slice(k * 128, (k + 1) * 128)
             w = pa[h, rows, :].astype(F32) * (acf[k, 0:1, :] * inverse)
             pa[h, rows, :] = w.astype(BF16)
             dsa[rows, :] = (w * (dpa[h, rows, :] - delta)).astype(BF16)
-            return carry
-
-        lax.fori_loop(0, n_z, one, 0)
         low = pa[h]
         ds = dsa[...]
         dk = mm(ds, qn[:, cols], NN) * unscale
@@ -388,26 +378,15 @@
         vout[:, cols] = mm(g[1, :, cols], low, TN).T.astype(BF16)
         dvid[0, :, cols] = mm(gkn[:, cols], ds, TN).T * scale
 
-    tile = 256
-    tiles = arows // tile
-
     def audio_second(h):
         cols = head_cols(h)
 
-        def one(t, carry):
-            lanes = aligned(t * tile, tile, tile)
-
-            def stat(ref, at):
-                return jnp.concatenate([ref[t * 2, at : at + 1, :], ref[t * 2 + 1, at : at + 1, :]], axis=1)
-
-            coef = jnp.exp2(stat(sloc, h) - stat(sall, h))
-            delta = stat(sall, 3 + h)
+        for k in range(n_z):
+            lanes = slice(k * HD, (k + 1) * HD)
+            coef = jnp.exp2(sloc[k, h : h + 1, :] - sall[k, h : h + 1, :])
             w = pb[h, :, lanes].astype(F32) * coef
             pb[h, :, lanes] = w.astype(BF16)
-            dsb[:, lanes] = (w * (dpb[h, :, lanes] - delta)).astype(BF16)
-            return carry
-
-        lax.fori_loop(0, tiles, one, 0)
+            dsb[:, lanes] = (w * (dpb[h, :, lanes] - sall[k, 3 + h : 4 + h, :])).astype(BF16)
         low = pb[h]
         ds = dsb[...]
         part[HEADS + h, :, 0:HD] = mm(raw_v[2, :, cols], low, TN).T.astype(BF16)
@@ -419,8 +398,8 @@
         dvid[1, :, cols] = mm(ds, gqn[:, cols], NN) * unscale
         vvg[:, cols] = mm(low, g[0, :, cols], NN).astype(BF16)
 
-    over_first = (0, HEADS + 1, HEADS + 2)
-    mirrored = (0, 2, HEADS + 2)
+    over_first = (3, 4, 5)
+    mirrored = (1, 3, 5)
     rchain = {}
     order = []
     for dist in range(nr, 0, -1):
@@ -490,22 +469,17 @@
     def steps(*what):
         scatter_step(*[(u, k) for u, k in what if k < nr])
 
-    video_second(0)
-    scatter_over(0)
-    video_second(1)
-    steps((1, 0))
-    video_second(2)
-    steps((2, 0))
-    steps((0, 0))
+    for h in range(HEADS):
+        video_second(h)
+        steps((h, 0))
     for copy in stat2:
         copy.wait_recv()
     audio_second(0)
-    steps((3, 0), (1, 1), (2, 1), (0, 1))
+    scatter_over(3)
     audio_second(1)
-    scatter_over(4)
     audio_second(2)
-    scatter_over(5)
-    steps((3, 1), (1, 2), (2, 2), (0, 2))
+    scatter_over(4, 5)
+    steps((0, 1), (1, 1), (2, 1), (3, 0))
 
     for n, row in ((0, 0), (1, 3)):
         inner = dvid[n] * (qn, kn)[n][...].astype(F32) * (1.0 / c if n == 0 else 1.0)
@@ -534,7 +508,7 @@
 
     write(vout, vo_h)
     write(vvg, vvg_h)
-    steps((4, 0), (5, 0), (1, 3), (2, 3), (3, 2), (0, 3), (4, 1), (5, 1))
+    steps((0, 2), (1, 2), (2, 2), (3, 1), (4, 0), (5, 0))
 
     inner = tower_sum(1, exch) * (1.0 / depth)
 
@@ -551,7 +525,7 @@
         write((qn, kn)[n], (vqg_h, vkg_h)[n])
 
     video_grad(0)
-    steps((3, 3), (4, 2), (5, 2))
+    steps((0, 3), (1, 3), (2, 3), (3, 2), (4, 1), (5, 1))
     for copy in ucopies:
         copy.wait_recv()
     total = uin[0]
@@ -560,9 +534,9 @@
     small[2, t_at, 0:8, :] = total
     uexch = tower_start(2)
     video_grad(1)
-    scatter_cross(1, 2)
-    steps((4, 3), (5, 3))
-    scatter_cross(3)
+    steps((3, 3))
+    scatter_cross(0, 1, 2)
+    steps((4, 2), (5, 2))
     for copy in gcopies:
         copy.wait_recv()
     total = gbuf[0]
@@ -571,6 +545,7 @@
     if n_dp > 1:
         dbuf[d_at] = total
         gcopy = send(dbuf.at[d_at], dbuf.at[d_at], ds_.at[0], dr_.at[0], dp=1 - d_at)
+    steps((4, 3), (5, 3))
     uall = tower_sum(2, uexch) * (1.0 / depth)
     for n in range(2):
         ucol[n] = column_of(uall[n : n + 1, :])
@@ -680,7 +655,7 @@
                 full(2, 8, WIDTH),
                 full(4, WIDTH),
                 low(4, 64, WIDTH),
-                dma(8), dma(4, n_z), dma(4, n_z), dma(2, n_z), dma(2, n_z), dma(3, n_tower), dma(3, n_tower),
+                dma(8), dma(6, n_z), dma(6, n_z), dma(4, n_z), dma(4, n_z), dma(3, n_tower), dma(3, n_tower),
                 dma(n_seq), dma(n_seq), dma(n_seq), dma(n_seq), dma(n_z), dma(n_z), dma(n_seq), dma(n_seq),
                 dma(n_seq), dma(n_seq), dma(1), dma(1), dma(6, n_z), dma(6, n_z), dma(6, n_z), dma(6, n_z), dma(9),
             ],

time: 94.3 us -> 95 us (level)
  Pallas kernels: 91.4 us -> 92.8 us
    pallas_call x1, Pallas kernels: 88.6 us -> 90 us  [body(): pl.pallas_call(functools.partial(kernel, sizes), out_shape=shapes, in_spe...]
where the time goes in v4:
time: 95 us; the launch traced here: 94.9 us
  Pallas kernels  92.8 us (98%)
  between operations  2.11 us (2%)
    pallas_call x1, Pallas kernels, body(): pl.pallas_call(functools.partial(kernel, sizes), out_shape=shapes, in_spe...  90 us
    pallas_call x1, Pallas kernels, body(): pl.pallas_call(hand_over, out_shape=shapes, in_specs=[vmem] * 9, out_spec...  2.75 us

profile of v4, /device:TPU:8, one launch (start us, length us, event | category | flops | bytes accessed | tf_op | source)
XLA Modules:
  0.0 94.9 jit_solution(18115922689948331722)
XLA Ops:
  1.9 90.0 %shard_map.178 = (bf16[512,384]{1,0:T(8,128)(2,1)}, bf16[64,384]{1,0:T(8,128)(2,1)}, bf16[512,384]{1,0:T(8,128)(2,1)}, bf16[64,384]{1,0:T(8,128)(2,1)}, bf16[64,...) custom-call(bf16[512,384]{1,0:T(8,128)(2,1)} %bitcast.16, ...), custom_call_target="tpu_custom_call" | custom-call | flops 4800000000 | bytes 4000000 | tf_op jit(solution)/shard_map/pallas_call | solution.py:610
  91.9 2.7 %shard_map.179 = (bf16[512,384]{1,0:T(8,128)(2,1)}, bf16[64,384]{1,0:T(8,128)(2,1)}, bf16[512,384]{1,0:T(8,128)(2,1)}, bf16[64,384]{1,0:T(8,128)(2,1)}, bf16[64,...) custom-call(bf16[512,384]{1,0:T(8,128)(2,1)} %get-tuple-element.27.r, ...), custom_call_target="tpu_custom_call" | custom-call | tf_op jit(solution)/shard_map/pallas_call | solution.py:667

commit v5 on v4

--- a/solution.py
+++ b/solution.py
@@ -122,12 +122,21 @@
         pl.semaphore_signal(barrier, inc=1, device_id={"dp": 1 - d_at}, device_id_type=MESH)
         peers += 1
 
+    for n in range(4):
+        loads[n].wait()
+
     def put_video(n, which, row):
         for k in range(4):
             small[n, t_at, which * 4 + k : which * 4 + k + 1, :] = row[:, k * HD : (k + 1) * HD]
 
-    for n in range(4):
-        loads[n].wait()
+    for n in range(3):
+        small[n, t_at] = jnp.zeros((16, HD), F32)
+    both = jnp.concatenate([g[2, own, :].astype(F32), g[3, own, :].astype(F32)], axis=0)
+    small[0, t_at, 8:9, :] = lanes_of(both * both)
+    for n in range(2):
+        loads[4 + n].wait()
+        widened = raw_v[n].astype(F32)
+        put_video(0, n, lanes_of(widened * widened))
     pl.semaphore_wait(barrier, peers)
 
     def tower_start(n):
@@ -188,25 +197,13 @@
             if k <= nr:
                 gather_step(n, k)
 
+    exch = tower_start(0)
     gather_over(2)
     gather_over(3)
     gather((0, 0), (1, 0), (2, 0), (3, 0))
     gather_over(0)
     gather_over(1)
 
-    def put_video(n, which, row):
-        for k in range(4):
-            small[n, t_at, which * 4 + k : which * 4 + k + 1, :] = row[:, k * HD : (k + 1) * HD]
-
-    for n in range(3):
-        small[n, t_at] = jnp.zeros((16, HD), F32)
-    both = jnp.concatenate([g[2, own, :].astype(F32), g[3, own, :].astype(F32)], axis=0)
-    small[0, t_at, 8:9, :] = lanes_of(both * both)
-    for n in range(2):
-        loads[4 + n].wait()
-        widened = raw_v[n].astype(F32)
-        put_video(0, n, lanes_of(widened * widened))
-    exch = tower_start(0)
     gather((4, 0), (5, 0), (0, 1), (1, 1))
     sloc[...] = jnp.zeros_like(sloc)
     sres[...] = jnp.zeros_like(sres)
@@ -315,9 +312,9 @@
     gather((2, 1), (3, 1))
     rba[...] = column_of(factors[8:9, :])
     factor_video(factors)
-    gather((4, 1), (5, 1), (0, 2), (1, 2))
+    gather((4, 1), (5, 1), (0, 2), (1, 2), (2, 2), (3, 2))
     audio_first(0)
-    gather((2, 2), (3, 2), (4, 2), (5, 2), (0, 3), (1, 3))
+    gather((4, 2), (5, 2), (0, 3), (1, 3))
     both_ways(audio_first, 1)
     video_first(0)
     gather((2, 3), (3, 3), (0, 4), (1, 4), (4, 3), (5, 3))
@@ -329,21 +326,6 @@
     gather((2, 4), (3, 4))
     both_ways(video_first, 3)
 
-    for copy in stat1:
-        copy.wait_recv()
-    mx = sin[0, 0:3, :]
-    for k in range(1, n_seq):
-        mx = jnp.maximum(mx, sin[k, 0:3, :])
-    tot = jnp.zeros((3, HD), F32)
-    inn = jnp.zeros((3, HD), F32)
-    for k in range(n_seq):
-        f = jnp.exp2(sin[k, 0:3, :] - mx)
-        tot = tot + sin[k, 3:6, :] * f
-        inn = inn + sin[k, 6:9, :] * f
-    sres[0:3, :] = mx + jnp.log2(tot)
-    sres[3:6, :] = inn / tot
-    stat2 = [send(sres, sall.at[z], s2s.at[k], s2r.at[k], seq=seq_id(x, z + k)) for k in range(1, n_z)]
-    sall[z] = sres[...]
     gather((4, 4), (5, 4))
     both_ways(video_first, 4)
 
@@ -398,8 +380,8 @@
         dvid[1, :, cols] = mm(ds, gqn[:, cols], NN) * unscale
         vvg[:, cols] = mm(low, g[0, :, cols], NN).astype(BF16)
 
-    over_first = (3, 4, 5)
-    mirrored = (1, 3, 5)
+    over_first = (0, 1, 5)
+    mirrored = (0, 3, 5)
     rchain = {}
     order = []
     for dist in range(nr, 0, -1):
@@ -469,17 +451,38 @@
     def steps(*what):
         scatter_step(*[(u, k) for u, k in what if k < nr])
 
-    for h in range(HEADS):
-        video_second(h)
-        steps((h, 0))
+    video_second(0)
+    scatter_over(0)
+    video_second(1)
+    scatter_over(1)
+    video_second(2)
+    steps((2, 0))
+
+    for copy in stat1:
+        copy.wait_recv()
+    mx = sin[0, 0:3, :]
+    for k in range(1, n_seq):
+        mx = jnp.maximum(mx, sin[k, 0:3, :])
+    tot = jnp.zeros((3, HD), F32)
+    inn = jnp.zeros((3, HD), F32)
+    for k in range(n_seq):
+        f = jnp.exp2(sin[k, 0:3, :] - mx)
+        tot = tot + sin[k, 3:6, :] * f
+        inn = inn + sin[k, 6:9, :] * f
+    sres[0:3, :] = mx + jnp.log2(tot)
+    sres[3:6, :] = inn / tot
+    stat2 = [send(sres, sall.at[z], s2s.at[k], s2r.at[k], seq=seq_id(x, z + k)) for k in range(1, n_z)]
+    sall[z] = sres[...]
+    steps((0, 0), (1, 0))
     for copy in stat2:
         copy.wait_recv()
     audio_second(0)
-    scatter_over(3)
+    steps((3, 0))
     audio_second(1)
+    steps((4, 0))
     audio_second(2)
-    scatter_over(4, 5)
-    steps((0, 1), (1, 1), (2, 1), (3, 0))
+    scatter_over(5)
+    steps((2, 1), (0, 1), (1, 1))
 
     for n, row in ((0, 0), (1, 3)):
         inner = dvid[n] * (qn, kn)[n][...].astype(F32) * (1.0 / c if n == 0 else 1.0)
@@ -508,8 +511,16 @@
 
     write(vout, vo_h)
     write(vvg, vvg_h)
-    steps((0, 2), (1, 2), (2, 2), (3, 1), (4, 0), (5, 0))
-
+    steps((3, 1), (4, 1), (2, 2), (0, 2), (1, 2), (5, 0))
+    steps((2, 3), (3, 2), (4, 2), (0, 3), (1, 3), (5, 1))
+    scatter_cross(2)
+    for copy in ucopies:
+        copy.wait_recv()
+    total = uin[0]
+    for k in range(1, n_seq):
+        total = total + uin[k]
+    small[2, t_at, 0:8, :] = total
+    uexch = tower_start(2)
     inner = tower_sum(1, exch) * (1.0 / depth)
 
     def video_grad(n):
@@ -525,18 +536,7 @@
         write((qn, kn)[n], (vqg_h, vkg_h)[n])
 
     video_grad(0)
-    steps((0, 3), (1, 3), (2, 3), (3, 2), (4, 1), (5, 1))
-    for copy in ucopies:
-        copy.wait_recv()
-    total = uin[0]
-    for k in range(1, n_seq):
-        total = total + uin[k]
-    small[2, t_at, 0:8, :] = total
-    uexch = tower_start(2)
-    video_grad(1)
-    steps((3, 3))
-    scatter_cross(0, 1, 2)
-    steps((4, 2), (5, 2))
+    steps((3, 3), (4, 3), (5, 2))
     for copy in gcopies:
         copy.wait_recv()
     total = gbuf[0]
@@ -545,7 +545,9 @@
     if n_dp > 1:
         dbuf[d_at] = total
         gcopy = send(dbuf.at[d_at], dbuf.at[d_at], ds_.at[0], dr_.at[0], dp=1 - d_at)
-    steps((4, 3), (5, 3))
+    video_grad(1)
+    steps((5, 3))
+    scatter_cross(3, 4)
     uall = tower_sum(2, uexch) * (1.0 / depth)
     for n in range(2):
         ucol[n] = column_of(uall[n : n + 1, :])
@@ -580,12 +582,16 @@
 
 
 def hand_over(*refs):
-    count = (len(refs) - 1) // 2
+    count = len(refs) // 3
     sems = refs[-1]
-    copies = [pltpu.make_async_copy(refs[n], refs[count + n], sems.at[n]) for n in range(count)]
-    for copy in copies:
+    ins = [pltpu.make_async_copy(refs[n], refs[2 * count + n], sems.at[0, n]) for n in range(count)]
+    outs = [pltpu.make_async_copy(refs[2 * count + n], refs[count + n], sems.at[1, n]) for n in range(count)]
+    for copy in ins:
         copy.start()
-    for copy in copies:
+    for n in range(count):
+        ins[n].wait()
+        outs[n].start()
+    for copy in outs:
         copy.wait()
 
 
@@ -667,9 +673,9 @@
         results = pl.pallas_call(
             hand_over,
             out_shape=shapes,
-            in_specs=[vmem] * 9,
+            in_specs=[any_spec] * 9,
             out_specs=tuple([any_spec] * 9),
-            scratch_shapes=[dma(9)],
+            scratch_shapes=[pltpu.VMEM(s.shape, s.dtype) for s in shapes] + [dma(2, 9)],
         )(*results)
         return tuple(r[None] for r in results[:8]) + (results[8],)
 

time: 95 us -> 93.6 us (0.985)
  Pallas kernels: 92.8 us -> 91.3 us
    pallas_call x1, Pallas kernels: 90 us -> 88.9 us  [body(): pl.pallas_call(functools.partial(kernel, sizes), out_shape=shapes, in_spe...]
where the time goes in v5:
time: 93.6 us; the launch traced here: 93.4 us
  Pallas kernels  91.3 us (98%)
  between operations  2.11 us (2%)
    pallas_call x1, Pallas kernels, body(): pl.pallas_call(functools.partial(kernel, sizes), out_shape=shapes, in_spe...  88.9 us
    pallas_call x1, Pallas kernels, body(): pl.pallas_call(hand_over, out_shape=shapes, in_specs=[any_spec] * 9, out_...  2.36 us

profile of v5, /device:TPU:8, one launch (start us, length us, event | category | flops | bytes accessed | tf_op | source)
XLA Modules:
  0.0 93.4 jit_solution(201203265575720982)
XLA Ops:
  1.9 88.9 %shard_map.178 = (bf16[512,384]{1,0:T(8,128)(2,1)}, bf16[64,384]{1,0:T(8,128)(2,1)}, bf16[512,384]{1,0:T(8,128)(2,1)}, bf16[64,384]{1,0:T(8,128)(2,1)}, bf16[64,...) custom-call(bf16[512,384]{1,0:T(8,128)(2,1)} %bitcast.16, ...), custom_call_target="tpu_custom_call" | custom-call | flops 4800000000 | bytes 4000000 | tf_op jit(solution)/shard_map/pallas_call | solution.py:616
  90.9 2.4 %shard_map.179 = (bf16[512,384]{1,0:T(8,128)(2,1)}, bf16[64,384]{1,0:T(8,128)(2,1)}, bf16[512,384]{1,0:T(8,128)(2,1)}, bf16[64,384]{1,0:T(8,128)(2,1)}, bf16[64,...) custom-call(bf16[512,384]{1,0:T(8,128)(2,1)} %get-tuple-element.27.r, ...), custom_call_target="tpu_custom_call" | custom-call | tf_op jit(solution)/shard_map/pallas_call | solution.py:673

commit v6 on v5

--- a/solution.py
+++ b/solution.py
@@ -49,6 +49,29 @@
 
 def wide(block, n):
     return jnp.concatenate([block] * n, axis=1)
+
+
+EVENTS = (
+    ("masks",), ("g", 0, 1, "l"), ("g", 0, 1, "s"), ("g", 1, 1, "s"), ("g", 1, 1, "l"), ("tower",),
+    ("g", 2, 1, "l"), ("g", 2, 1, "s"), ("vid",), ("g", 3, 1, "l"), ("g", 0, 2, "l"), ("g", 3, 1, "s"),
+    ("g", 0, 2, "s"), ("g", 1, 2, "s"), ("g", 1, 2, "l"), ("g0", 4), ("g0", 5), ("B1", 0), ("g", 2, 2, "l"),
+    ("g", 2, 2, "s"), ("B1", -1), ("g", 3, 2, "l"), ("g", 0, 3, "l"), ("B1", 1), ("A1", 0), ("g", 3, 2, "s"),
+    ("g", 0, 3, "s"), ("g", 1, 3, "l"), ("g", 1, 3, "s"), ("g", 4, 1, "s"), ("g", 4, 1, "l"), ("B1", -2),
+    ("g", 5, 1, "l"), ("g", 5, 1, "s"), ("B1", 2), ("A1", -1), ("g", 2, 3, "l"), ("g", 2, 3, "s"), ("A1", 1),
+    ("g", 3, 3, "l"), ("g", 0, 4, "l"), ("g", 1, 4, "l"), ("g", 3, 3, "s"), ("B1", 3), ("g", 4, 2, "s"),
+    ("g", 4, 2, "l"), ("B1", -3), ("g", 5, 2, "l"), ("g", 5, 2, "s"), ("A1", -2), ("A1", 2), ("g", 2, 4, "l"),
+    ("g", 3, 4, "l"), ("B1", -4), ("g", 4, 3, "s"), ("g", 4, 3, "l"), ("g", 5, 3, "l"), ("g", 5, 3, "s"),
+    ("A1", -3), ("A1", 3), ("g", 4, 4, "l"), ("stat1",), ("g", 5, 4, "l"), ("A1", -4), ("A2", 0), ("A2", 1),
+    ("A2", 2), ("stat2",), ("B2", 0), ("u", 0, 1, "l"), ("u", 0, 1, "s"), ("u", 1, 0, "l"), ("B2", 1), ("B2", 2),
+    ("u", 1, 0, "s"), ("u", 2, 1, "l"), ("u", 2, 1, "s"), ("inner",), ("u", 1, 1, "l"), ("u", 0, 2, "l"),
+    ("u", 4, 1, "l"), ("u", 0, 2, "s"), ("u", 1, 1, "s"), ("u", 3, 0, "l"), ("u", 4, 1, "s"), ("u", 2, 2, "l"),
+    ("u", 3, 0, "s"), ("u", 2, 2, "s"), ("u", 1, 2, "l"), ("u", 0, 3, "l"), ("usum",), ("gsum",), ("vg", 0),
+    ("u", 3, 1, "l"), ("u", 4, 2, "l"), ("u", 1, 2, "s"), ("vg", 1), ("u", 5, 0, "l"), ("u", 2, 3, "l"),
+    ("u", 4, 2, "s"), ("u", 5, 0, "s"), ("u", 3, 1, "s"), ("fin",), ("u", 1, 3, "l"), ("cross", 0),
+    ("u", 3, 2, "l"), ("u", 5, 1, "l"), ("u", 4, 3, "l"), ("end", 1), ("end", 0), ("cross", 2), ("u", 3, 3, "l"),
+    ("u", 5, 1, "s"), ("u", 5, 2, "l"), ("u", 3, 2, "s"), ("cross", 4), ("end", 2), ("u", 5, 2, "s"),
+    ("u", 5, 3, "l"), ("end", 3), ("end", 4), ("end", 5),
+)
 
 
 def kernel(
@@ -156,7 +179,7 @@
     arrays = (0, 2, 1, 3, 1, 3)
     chains = {}
 
-    def gather_step(n, k):
+    def gather_step(n, k, only=None):
         a = arrays[n]
         sign = 1 if n % 2 else -1
         ways = (("l", nr, left if n % 2 else right, sign, 0), ("s", nl, right if n % 2 else left, -sign, nr))
@@ -168,7 +191,7 @@
         if k == 0 and n >= 4:
             chains[n - 2, "x", 0].wait_recv()
         for name, count, to, way, base in ways:
-            if k > count:
+            if k > count or only not in (None, name):
                 continue
             here = block(z + way * k)
             if k > 0:
@@ -192,30 +215,26 @@
             at = nr + abs(delta)
         chains[n, "x", at].wait_recv()
 
-    def gather(*what):
-        for n, k in what:
-            if k <= nr:
-                gather_step(n, k)
-
     exch = tower_start(0)
-    gather_over(2)
-    gather_over(3)
-    gather((0, 0), (1, 0), (2, 0), (3, 0))
-    gather_over(0)
-    gather_over(1)
-
-    gather((4, 0), (5, 0), (0, 1), (1, 1))
+    for n in range(4):
+        if n > 1:
+            gather_over(n)
+        gather_step(n, 0)
+        if n < 2:
+            gather_over(n)
     sloc[...] = jnp.zeros_like(sloc)
     sres[...] = jnp.zeros_like(sres)
     ub[...] = jnp.zeros_like(ub)
     gbuf[s_at] = jnp.zeros((8, WIDTH), F32)
-    rho = lax.broadcasted_iota(jnp.int32, (arows, HD), 0)
-    token = ((rho // 64) % 2) * (n_z * 64) + (rho // 128) * 64 + rho % 64
-    bias_a[...] = jnp.where(token < alen[0], 0.0, MASKED)
-    vtok = s_at * VROWS + lax.broadcasted_iota(jnp.int32, (VROWS, HD), 0)
-    bias_v[...] = jnp.where(vtok < vlen[0], 0.0, MASKED)
     for n in (6, 7):
         loads[n].wait()
+
+    def masks():
+        rho = lax.broadcasted_iota(jnp.int32, (arows, HD), 0)
+        token = ((rho // 64) % 2) * (n_z * 64) + (rho // 128) * 64 + rho % 64
+        bias_a[...] = jnp.where(token < alen[0], 0.0, MASKED)
+        vtok = s_at * VROWS + lax.broadcasted_iota(jnp.int32, (VROWS, HD), 0)
+        bias_v[...] = jnp.where(vtok < vlen[0], 0.0, MASKED)
 
     everyone = [(delta, k) for delta in range(n_z) for k in range(2) if delta or k]
     fsent = {}
@@ -301,34 +320,6 @@
                     gain = gains[3 * n : 3 * n + 1, cols] * (c if n == 0 else 1.0)
                     (qn, kn)[n][rows, cols] = (raw_v[n, rows, cols].astype(F32) * col * gain).astype(BF16)
 
-    def both_ways(run, dist):
-        if dist < nr or dist <= nl:
-            run(-dist, dist)
-        elif dist == nr:
-            run(-dist)
-
-    factors = lax.rsqrt(tower_sum(0, exch) / depth + EPS)
-    factors_out(factors[8:9, :])
-    gather((2, 1), (3, 1))
-    rba[...] = column_of(factors[8:9, :])
-    factor_video(factors)
-    gather((4, 1), (5, 1), (0, 2), (1, 2), (2, 2), (3, 2))
-    audio_first(0)
-    gather((4, 2), (5, 2), (0, 3), (1, 3))
-    both_ways(audio_first, 1)
-    video_first(0)
-    gather((2, 3), (3, 3), (0, 4), (1, 4), (4, 3), (5, 3))
-    both_ways(video_first, 1)
-    both_ways(audio_first, 2)
-    both_ways(video_first, 2)
-    both_ways(audio_first, 3)
-    both_ways(audio_first, 4)
-    gather((2, 4), (3, 4))
-    both_ways(video_first, 3)
-
-    gather((4, 4), (5, 4))
-    both_ways(video_first, 4)
-
     def video_second(h):
         cols = head_cols(h)
         m = ast[h, 0, 0:1, :]
@@ -380,8 +371,8 @@
         dvid[1, :, cols] = mm(ds, gqn[:, cols], NN) * unscale
         vvg[:, cols] = mm(low, g[0, :, cols], NN).astype(BF16)
 
-    over_first = (0, 1, 5)
-    mirrored = (0, 3, 5)
+    over_first = (1, 3, 5)
+    mirrored = (0, 2, 4)
     rchain = {}
     order = []
     for dist in range(nr, 0, -1):
@@ -400,8 +391,8 @@
                     xi_s.at[u, k], xi_r.at[u, k], seq=over,
                 )
 
-    def scatter_step(*what):
-        for u, k in what:
+    def scatter_step(u, k, only):
+        if True:
             early = u in over_first
             way = -1 if u in mirrored else 1
             size = 64 if early else 128
@@ -409,7 +400,7 @@
             for name, n, to, sign, base, land in (
                 ("l", nr, ends[0], way, 0, rr), ("s", nl, ends[1], -way, nr, rl),
             ):
-                if k >= n:
+                if k >= n or name != only:
                     continue
                 delta = sign * (n - k)
                 at = ring(z + delta)
@@ -448,60 +439,79 @@
         rchain[u, "k"].wait_recv()
         return fin[u, aligned(x * 64, 64, 64), :] + xr[u].astype(F32)
 
-    def steps(*what):
-        scatter_step(*[(u, k) for u, k in what if k < nr])
-
-    video_second(0)
-    scatter_over(0)
-    video_second(1)
-    scatter_over(1)
-    video_second(2)
-    steps((2, 0))
-
-    for copy in stat1:
-        copy.wait_recv()
-    mx = sin[0, 0:3, :]
-    for k in range(1, n_seq):
-        mx = jnp.maximum(mx, sin[k, 0:3, :])
-    tot = jnp.zeros((3, HD), F32)
-    inn = jnp.zeros((3, HD), F32)
-    for k in range(n_seq):
-        f = jnp.exp2(sin[k, 0:3, :] - mx)
-        tot = tot + sin[k, 3:6, :] * f
-        inn = inn + sin[k, 6:9, :] * f
-    sres[0:3, :] = mx + jnp.log2(tot)
-    sres[3:6, :] = inn / tot
-    stat2 = [send(sres, sall.at[z], s2s.at[k], s2r.at[k], seq=seq_id(x, z + k)) for k in range(1, n_z)]
-    sall[z] = sres[...]
-    steps((0, 0), (1, 0))
-    for copy in stat2:
-        copy.wait_recv()
-    audio_second(0)
-    steps((3, 0))
-    audio_second(1)
-    steps((4, 0))
-    audio_second(2)
-    scatter_over(5)
-    steps((2, 1), (0, 1), (1, 1))
-
-    for n, row in ((0, 0), (1, 3)):
-        inner = dvid[n] * (qn, kn)[n][...].astype(F32) * (1.0 / c if n == 0 else 1.0)
-        put_video(1, n, lanes_of(inner))
-        gbuf[s_at, row : row + 1, :] = jnp.sum(inner, axis=0, keepdims=True) / gains[row : row + 1, :]
-    exch = tower_start(1)
-    for n in range(2):
-        row = lanes_of(acc[n])
-        for k in range(n_z):
-            ub[k, n : n + 1, :] = row[:, k * HD : (k + 1) * HD]
-    ucopies = []
-    for k in range(1, n_seq):
-        to = lax.rem(s_at + k, n_seq)
-        ucopies.append(send(ub.at[lax.rem(to, n_z)], uin.at[s_at], us.at[k], ur.at[k], seq=to))
-    uin[s_at] = ub[z]
-    gcopies = [
-        send(gbuf.at[s_at], gbuf.at[s_at], ggs.at[k], ggr.at[k], seq=lax.rem(s_at + k, n_seq))
-        for k in range(1, n_seq)
-    ]
+    def scatter_start(u):
+        if u in over_first:
+            scatter_over(u)
+        else:
+            scatter_step(u, 0, "l")
+            scatter_step(u, 0, "s")
+
+    state = {}
+
+    def combine():
+        for copy in stat1:
+            copy.wait_recv()
+        mx = sin[0, 0:3, :]
+        for k in range(1, n_seq):
+            mx = jnp.maximum(mx, sin[k, 0:3, :])
+        tot = jnp.zeros((3, HD), F32)
+        inn = jnp.zeros((3, HD), F32)
+        for k in range(n_seq):
+            f = jnp.exp2(sin[k, 0:3, :] - mx)
+            tot = tot + sin[k, 3:6, :] * f
+            inn = inn + sin[k, 6:9, :] * f
+        sres[0:3, :] = mx + jnp.log2(tot)
+        sres[3:6, :] = inn / tot
+        state["stat2"] = [send(sres, sall.at[z], s2s.at[k], s2r.at[k], seq=seq_id(x, z + k)) for k in range(1, n_z)]
+        sall[z] = sres[...]
+
+    def inner_products():
+        for n, row in ((0, 0), (1, 3)):
+            inner = dvid[n] * (qn, kn)[n][...].astype(F32) * (1.0 / c if n == 0 else 1.0)
+            put_video(1, n, lanes_of(inner))
+            gbuf[s_at, row : row + 1, :] = jnp.sum(inner, axis=0, keepdims=True) / gains[row : row + 1, :]
+        state["video"] = tower_start(1)
+        for n in range(2):
+            row = lanes_of(acc[n])
+            for k in range(n_z):
+                ub[k, n : n + 1, :] = row[:, k * HD : (k + 1) * HD]
+        state["u"] = []
+        state["g"] = []
+        for k in range(1, n_seq):
+            to = lax.rem(s_at + k, n_seq)
+            state["u"].append(send(ub.at[lax.rem(to, n_z)], uin.at[s_at], us.at[k], ur.at[k], seq=to))
+        uin[s_at] = ub[z]
+        for k in range(1, n_seq):
+            to = lax.rem(s_at + k, n_seq)
+            state["g"].append(send(gbuf.at[s_at], gbuf.at[s_at], ggs.at[k], ggr.at[k], seq=to))
+        write(vout, vo_h)
+        write(vvg, vvg_h)
+
+    def total_of(copies, ref):
+        for copy in copies:
+            copy.wait_recv()
+        total = ref[0]
+        for k in range(1, n_seq):
+            total = total + ref[k]
+        return total
+
+    def audio_inner():
+        small[2, t_at, 0:8, :] = total_of(state["u"], uin)
+        state["audio"] = tower_start(2)
+
+    def gain_sums():
+        dbuf[d_at] = total_of(state["g"], gbuf)
+        if n_dp > 1:
+            state["dp"] = send(dbuf.at[d_at], dbuf.at[d_at], ds_.at[0], dr_.at[0], dp=1 - d_at)
+
+    def gain_out():
+        if n_dp > 1:
+            state["dp"].wait_recv()
+            gout[...] = dbuf[0, 0:4, :] + dbuf[1, 0:4, :]
+        else:
+            gout[...] = dbuf[d_at, 0:4, :]
+        write(gout, gg_h)
+
     outs = []
 
     def write(src, dst):
@@ -509,25 +519,13 @@
         copy.start()
         outs.append(copy)
 
-    write(vout, vo_h)
-    write(vvg, vvg_h)
-    steps((3, 1), (4, 1), (2, 2), (0, 2), (1, 2), (5, 0))
-    steps((2, 3), (3, 2), (4, 2), (0, 3), (1, 3), (5, 1))
-    scatter_cross(2)
-    for copy in ucopies:
-        copy.wait_recv()
-    total = uin[0]
-    for k in range(1, n_seq):
-        total = total + uin[k]
-    small[2, t_at, 0:8, :] = total
-    uexch = tower_start(2)
-    inner = tower_sum(1, exch) * (1.0 / depth)
-
     def video_grad(n):
+        if n == 0:
+            state["inner"] = tower_sum(1, state["video"]) * (1.0 / depth)
         row = 3 * n
         for k in range(4):
             rows = slice(k * HD, (k + 1) * HD)
-            col = column_of(inner[n * 4 + k : n * 4 + k + 1, :])
+            col = column_of(state["inner"][n * 4 + k : n * 4 + k + 1, :])
             r = rbv[n, rows, :]
             for h in range(HEADS):
                 cols = head_cols(h)
@@ -535,46 +533,82 @@
                 (qn, kn)[n][rows, cols] = grad.astype(BF16)
         write((qn, kn)[n], (vqg_h, vkg_h)[n])
 
-    video_grad(0)
-    steps((3, 3), (4, 3), (5, 2))
-    for copy in gcopies:
-        copy.wait_recv()
-    total = gbuf[0]
-    for k in range(1, n_seq):
-        total = total + gbuf[k]
-    if n_dp > 1:
-        dbuf[d_at] = total
-        gcopy = send(dbuf.at[d_at], dbuf.at[d_at], ds_.at[0], dr_.at[0], dp=1 - d_at)
-    video_grad(1)
-    steps((5, 3))
-    scatter_cross(3, 4)
-    uall = tower_sum(2, uexch) * (1.0 / depth)
-    for n in range(2):
-        ucol[n] = column_of(uall[n : n + 1, :])
-
     def audio_grad(n, h, total):
         cols = head_cols(h)
         r = rba[(1 - n) * 64 : (2 - n) * 64, :]
         col = ucol[n, aligned(x * 64, 64, 64), :]
         return (r * gains[n + 1 : n + 2, cols] * total - g[3 - n, own, cols].astype(F32) * (r * r * col)).astype(BF16)
 
-    if n_dp > 1:
-        gcopy.wait_recv()
-        total = dbuf[0] + dbuf[1]
-    gout[...] = total[0:4, :]
-    write(gout, gg_h)
-    for h in range(HEADS):
-        both = scatter_end(h)
-        outa[2, :, head_cols(h)] = audio_grad(0, h, both[:, 0:HD])
-        outa[3, :, head_cols(h)] = both[:, HD:].astype(BF16)
-    write(outa.at[2], akg_h)
-    write(outa.at[3], avg_h)
-    for h in range(HEADS):
-        both = scatter_end(HEADS + h)
-        outa[0, :, head_cols(h)] = both[:, 0:HD].astype(BF16)
-        outa[1, :, head_cols(h)] = audio_grad(1, h, both[:, HD:])
-    write(outa.at[0], aco_h)
-    write(outa.at[1], aqg_h)
+    ended = []
+
+    def unit_end(u):
+        if not ended:
+            uall = tower_sum(2, state["audio"]) * (1.0 / depth)
+            for n in range(2):
+                ucol[n] = column_of(uall[n : n + 1, :])
+        both = scatter_end(u)
+        h = u % HEADS
+        if u < HEADS:
+            outa[2, :, head_cols(h)] = audio_grad(0, h, both[:, 0:HD])
+            outa[3, :, head_cols(h)] = both[:, HD:].astype(BF16)
+        else:
+            outa[0, :, head_cols(h)] = both[:, 0:HD].astype(BF16)
+            outa[1, :, head_cols(h)] = audio_grad(1, h, both[:, HD:])
+        ended.append(u)
+        for first, parts in ((0, ((2, akg_h), (3, avg_h))), (HEADS, ((0, aco_h), (1, aqg_h)))):
+            if first <= u < first + HEADS and all(first + k in ended for k in range(HEADS)):
+                for n, dst in parts:
+                    write(outa.at[n], dst)
+
+    def tower_factors():
+        state["factors"] = lax.rsqrt(tower_sum(0, exch) / depth + EPS)
+        factors_out(state["factors"][8:9, :])
+        rba[...] = column_of(state["factors"][8:9, :])
+
+    reach = {"l": nr, "s": nl}
+    for what, *at in EVENTS:
+        if what == "g0":
+            gather_step(at[0], 0)
+        elif what == "g":
+            if at[1] <= reach[at[2]]:
+                gather_step(*at)
+        elif what == "masks":
+            masks()
+        elif what == "tower":
+            tower_factors()
+        elif what == "vid":
+            factor_video(state["factors"])
+        elif what in ("A1", "B1"):
+            if -nr <= at[0] <= nl:
+                (video_first if what == "A1" else audio_first)(at[0])
+        elif what == "A2":
+            video_second(at[0])
+            scatter_start(at[0])
+        elif what == "B2":
+            audio_second(at[0])
+            scatter_start(HEADS + at[0])
+        elif what == "stat1":
+            combine()
+        elif what == "stat2":
+            for copy in state["stat2"]:
+                copy.wait_recv()
+        elif what == "u":
+            if at[1] < reach[at[2]]:
+                scatter_step(*at)
+        elif what == "cross":
+            scatter_cross(at[0])
+        elif what == "inner":
+            inner_products()
+        elif what == "usum":
+            audio_inner()
+        elif what == "gsum":
+            gain_sums()
+        elif what == "vg":
+            video_grad(at[0])
+        elif what == "fin":
+            gain_out()
+        else:
+            unit_end(at[0])
     for copy in outs:
         copy.wait()
     for copy in pending:

time: 93.6 us -> 89.9 us (0.960)
  Pallas kernels: 91.3 us -> 87.6 us
    pallas_call x1, Pallas kernels: 88.9 us -> 85.3 us  [body(): pl.pallas_call(functools.partial(kernel, sizes), out_shape=shapes, in_spe...]
where the time goes in v6:
time: 89.9 us; the launch traced here: 89.8 us
  Pallas kernels  87.6 us (97%)
  between operations  2.11 us (2%)
    pallas_call x1, Pallas kernels, body(): pl.pallas_call(functools.partial(kernel, sizes), out_shape=shapes, in_spe...  85.3 us
    pallas_call x1, Pallas kernels, body(): pl.pallas_call(hand_over, out_shape=shapes, in_specs=[any_spec] * 9, out_...  2.36 us

profile of v6, /device:TPU:8, one launch (start us, length us, event | category | flops | bytes accessed | tf_op | source)
XLA Modules:
  0.0 89.8 jit_solution(7532824825113826124)
XLA Ops:
  1.9 85.3 %shard_map.178 = (bf16[512,384]{1,0:T(8,128)(2,1)}, bf16[64,384]{1,0:T(8,128)(2,1)}, bf16[512,384]{1,0:T(8,128)(2,1)}, bf16[64,384]{1,0:T(8,128)(2,1)}, bf16[64,...) custom-call(bf16[512,384]{1,0:T(8,128)(2,1)} %bitcast.16, ...), custom_call_target="tpu_custom_call" | custom-call | flops 4800000000 | bytes 4000000 | tf_op jit(solution)/shard_map/pallas_call | solution.py:650
  87.2 2.4 %shard_map.179 = (bf16[512,384]{1,0:T(8,128)(2,1)}, bf16[64,384]{1,0:T(8,128)(2,1)}, bf16[512,384]{1,0:T(8,128)(2,1)}, bf16[64,384]{1,0:T(8,128)(2,1)}, bf16[64,...) custom-call(bf16[512,384]{1,0:T(8,128)(2,1)} %get-tuple-element.27.r, ...), custom_call_target="tpu_custom_call" | custom-call | tf_op jit(solution)/shard_map/pallas_call | solution.py:707

commit v7 on v6

--- a/solution.py
+++ b/solution.py
@@ -52,25 +52,24 @@
 
 
 EVENTS = (
-    ("masks",), ("g", 0, 1, "l"), ("g", 0, 1, "s"), ("g", 1, 1, "s"), ("g", 1, 1, "l"), ("tower",),
-    ("g", 2, 1, "l"), ("g", 2, 1, "s"), ("vid",), ("g", 3, 1, "l"), ("g", 0, 2, "l"), ("g", 3, 1, "s"),
-    ("g", 0, 2, "s"), ("g", 1, 2, "s"), ("g", 1, 2, "l"), ("g0", 4), ("g0", 5), ("B1", 0), ("g", 2, 2, "l"),
-    ("g", 2, 2, "s"), ("B1", -1), ("g", 3, 2, "l"), ("g", 0, 3, "l"), ("B1", 1), ("A1", 0), ("g", 3, 2, "s"),
-    ("g", 0, 3, "s"), ("g", 1, 3, "l"), ("g", 1, 3, "s"), ("g", 4, 1, "s"), ("g", 4, 1, "l"), ("B1", -2),
-    ("g", 5, 1, "l"), ("g", 5, 1, "s"), ("B1", 2), ("A1", -1), ("g", 2, 3, "l"), ("g", 2, 3, "s"), ("A1", 1),
-    ("g", 3, 3, "l"), ("g", 0, 4, "l"), ("g", 1, 4, "l"), ("g", 3, 3, "s"), ("B1", 3), ("g", 4, 2, "s"),
-    ("g", 4, 2, "l"), ("B1", -3), ("g", 5, 2, "l"), ("g", 5, 2, "s"), ("A1", -2), ("A1", 2), ("g", 2, 4, "l"),
-    ("g", 3, 4, "l"), ("B1", -4), ("g", 4, 3, "s"), ("g", 4, 3, "l"), ("g", 5, 3, "l"), ("g", 5, 3, "s"),
-    ("A1", -3), ("A1", 3), ("g", 4, 4, "l"), ("stat1",), ("g", 5, 4, "l"), ("A1", -4), ("A2", 0), ("A2", 1),
-    ("A2", 2), ("stat2",), ("B2", 0), ("u", 0, 1, "l"), ("u", 0, 1, "s"), ("u", 1, 0, "l"), ("B2", 1), ("B2", 2),
-    ("u", 1, 0, "s"), ("u", 2, 1, "l"), ("u", 2, 1, "s"), ("inner",), ("u", 1, 1, "l"), ("u", 0, 2, "l"),
-    ("u", 4, 1, "l"), ("u", 0, 2, "s"), ("u", 1, 1, "s"), ("u", 3, 0, "l"), ("u", 4, 1, "s"), ("u", 2, 2, "l"),
-    ("u", 3, 0, "s"), ("u", 2, 2, "s"), ("u", 1, 2, "l"), ("u", 0, 3, "l"), ("usum",), ("gsum",), ("vg", 0),
-    ("u", 3, 1, "l"), ("u", 4, 2, "l"), ("u", 1, 2, "s"), ("vg", 1), ("u", 5, 0, "l"), ("u", 2, 3, "l"),
-    ("u", 4, 2, "s"), ("u", 5, 0, "s"), ("u", 3, 1, "s"), ("fin",), ("u", 1, 3, "l"), ("cross", 0),
-    ("u", 3, 2, "l"), ("u", 5, 1, "l"), ("u", 4, 3, "l"), ("end", 1), ("end", 0), ("cross", 2), ("u", 3, 3, "l"),
-    ("u", 5, 1, "s"), ("u", 5, 2, "l"), ("u", 3, 2, "s"), ("cross", 4), ("end", 2), ("u", 5, 2, "s"),
-    ("u", 5, 3, "l"), ("end", 3), ("end", 4), ("end", 5),
+    ("masks",), ("g", 0, 1, "l"), ("g", 0, 1, "s"), ("g", 1, 1, "s"), ("g", 1, 1, "l"), ("tower",), ("vid",),
+    ("g0", 4), ("g0", 5), ("g", 2, 1, "l"), ("g", 3, 1, "l"), ("g", 2, 1, "s"), ("g", 3, 1, "s"), ("g", 0, 2, "l"),
+    ("g", 0, 2, "s"), ("g", 1, 2, "s"), ("g", 1, 2, "l"), ("B1", 0), ("g", 4, 1, "l"), ("g", 4, 1, "s"), ("B1", -1),
+    ("B1", 1), ("g", 5, 1, "l"), ("g", 5, 1, "s"), ("A1", 0), ("g", 2, 2, "l"), ("g", 3, 2, "l"), ("A1", -1),
+    ("A1", 1), ("g", 2, 2, "s"), ("g", 3, 2, "s"), ("B1", -2), ("g", 0, 3, "l"), ("g", 0, 3, "s"), ("B1", 2),
+    ("g", 1, 3, "s"), ("g", 1, 3, "l"), ("g", 4, 2, "l"), ("g", 4, 2, "s"), ("g", 5, 2, "s"), ("g", 5, 2, "l"),
+    ("A1", -2), ("A1", 2), ("g", 2, 3, "l"), ("g", 3, 3, "l"), ("g", 3, 3, "s"), ("g", 2, 3, "s"), ("B1", -3),
+    ("g", 0, 4, "l"), ("g", 1, 4, "l"), ("B1", 3), ("g", 4, 3, "l"), ("g", 4, 3, "s"), ("g", 5, 3, "s"),
+    ("g", 5, 3, "l"), ("A1", -3), ("A1", 3), ("g", 2, 4, "l"), ("g", 3, 4, "l"), ("g", 4, 4, "l"), ("B1", -4),
+    ("g", 5, 4, "l"), ("A1", -4), ("A2", 0), ("A2", 1), ("A2", 2), ("stat1",), ("u", 0, 1, "l"), ("u", 0, 1, "s"),
+    ("u", 1, 1, "s"), ("u", 1, 1, "l"), ("u", 2, 1, "l"), ("u", 2, 1, "s"), ("u", 0, 2, "l"), ("u", 0, 2, "s"),
+    ("stat2",), ("B2", 0), ("u", 1, 2, "s"), ("u", 1, 2, "l"), ("B2", 1), ("u", 2, 2, "l"), ("u", 2, 2, "s"),
+    ("B2", 2), ("u", 0, 3, "l"), ("u", 3, 0, "l"), ("inner",), ("u", 3, 0, "s"), ("u", 1, 3, "l"), ("u", 4, 1, "s"),
+    ("u", 4, 1, "l"), ("u", 2, 3, "l"), ("u", 3, 1, "l"), ("cross", 0), ("u", 5, 0, "l"), ("u", 3, 1, "s"),
+    ("cross", 1), ("u", 5, 0, "s"), ("usum",), ("u", 4, 2, "l"), ("u", 4, 2, "s"), ("gsum",), ("u", 3, 2, "l"),
+    ("vg", 0), ("cross", 2), ("u", 5, 1, "l"), ("vg", 1), ("u", 5, 1, "s"), ("u", 3, 2, "s"), ("u", 4, 3, "l"),
+    ("fin",), ("u", 3, 3, "l"), ("u", 5, 2, "l"), ("end", 0), ("end", 1), ("end", 2), ("u", 5, 2, "s"),
+    ("cross", 4), ("u", 5, 3, "l"), ("end", 3), ("end", 4), ("end", 5),
 )
 
 
@@ -371,8 +370,8 @@
         dvid[1, :, cols] = mm(ds, gqn[:, cols], NN) * unscale
         vvg[:, cols] = mm(low, g[0, :, cols], NN).astype(BF16)
 
-    over_first = (1, 3, 5)
-    mirrored = (0, 2, 4)
+    over_first = (3, 5)
+    mirrored = (0, 2, 5)
     rchain = {}
     order = []
     for dist in range(nr, 0, -1):

time: 89.9 us -> 88.6 us (0.986)
  Pallas kernels: 87.6 us -> 86.3 us
    pallas_call x1, Pallas kernels: 85.3 us -> 84 us  [body(): pl.pallas_call(functools.partial(kernel, sizes), out_shape=shapes, in_spe...]
where the time goes in v7:
time: 88.6 us; the launch traced here: 88.4 us
  Pallas kernels  86.3 us (97%)
  between operations  2.11 us (2%)
    pallas_call x1, Pallas kernels, body(): pl.pallas_call(functools.partial(kernel, sizes), out_shape=shapes, in_spe...  84 us
    pallas_call x1, Pallas kernels, body(): pl.pallas_call(hand_over, out_shape=shapes, in_specs=[any_spec] * 9, out_...  2.36 us

profile of v7, /device:TPU:8, one launch (start us, length us, event | category | flops | bytes accessed | tf_op | source)
XLA Modules:
  0.0 88.4 jit_solution(14973316501059546862)
XLA Ops:
  1.9 84.0 %shard_map.178 = (bf16[512,384]{1,0:T(8,128)(2,1)}, bf16[64,384]{1,0:T(8,128)(2,1)}, bf16[512,384]{1,0:T(8,128)(2,1)}, bf16[64,384]{1,0:T(8,128)(2,1)}, bf16[64,...) custom-call(bf16[512,384]{1,0:T(8,128)(2,1)} %bitcast.16, ...), custom_call_target="tpu_custom_call" | custom-call | flops 4800000000 | bytes 4000000 | tf_op jit(solution)/shard_map/pallas_call | solution.py:649
  85.9 2.4 %shard_map.179 = (bf16[512,384]{1,0:T(8,128)(2,1)}, bf16[64,384]{1,0:T(8,128)(2,1)}, bf16[512,384]{1,0:T(8,128)(2,1)}, bf16[64,384]{1,0:T(8,128)(2,1)}, bf16[64,...) custom-call(bf16[512,384]{1,0:T(8,128)(2,1)} %get-tuple-element.27.r, ...), custom_call_target="tpu_custom_call" | custom-call | tf_op jit(solution)/shard_map/pallas_call | solution.py:706
